TPU v7x, 256 devices: a whole 4x4x8 slice. The times are simulated.
256 devices in a mesh: dp: 32 (over z, x), col: 8 (over y, core).
Axes of the slice: x: 4, y: 4, z: 8, core: 2. Of those that a mesh axis runs over, the one named last changes fastest.
Arguments:
- grads: bfloat16 [32, 32768, 512], P('dp', 'col'), may hold values from -8 to 8
- momentum: float32 [32768, 512], P(('col', 'dp')), may hold values from -6 to 6
- weight: float32 [32768, 512], P(('col', 'dp')), may hold values from -0.3125 to 0.3125
- max_logits: int32 [32, 2, 64], P('dp'), may hold values from 0 to 3200, as said below
- threshold: int32 [1], replicated, may hold values from 1200 to 2000
Outputs:
- new_master: float32 [32768, 512], P(('col', 'dp'))
- new_momentum: float32 [32768, 512], P(('col', 'dp'))
- new_weight: bfloat16 [32768, 512], P('col')
- blend_rms: float32 [8], P('col')
Inputs may be any that keep to these rules, and one draw needn't show every extreme that they name: `max_logits`: in each layer, every head's largest value over the replicas is held by one replica; each replica holds it for 2 heads. Every value is 400 or more for at least one replica.
All inputs are finite; a program needn't handle non-finite values.
Results may differ from a plain program's by a relative error of at most 0.00045.
Values may be sent and summed in bfloat16 or wider, within the bound.
A program may use at most 64 MiB of HBM per device.

v0:
```python
import jax
import jax.numpy as jnp
from jax import lax
from jax.sharding import PartitionSpec as P

R = 512
HEADS = 64
NOPE = 128
VDIM = 128
ITERS = 5
LAYERS = 2
F = 16384


momentum_rate = 0.95
epsilon = 1e-07
coef_one = 3.4445
coef_two = -4.775
coef_three = 2.0315
learn_rate = 0.02
decay_rate = 0.1


def from_partner(value, axis, distance):
    mask = 2**distance
    pairs = [(source, source ^ mask) for source in range(lax.axis_size(axis))]
    return lax.ppermute(value, axis, pairs)


def product(left, right):
    return jnp.dot(left, right, precision=lax.Precision.HIGHEST, preferred_element_type=jnp.float32)


def group_gram(rows_block, span_bits):
    total = lax.psum(product(rows_block.T, rows_block), "dp")
    for bit in range(span_bits):
        total = total + from_partner(total, "col", bit)
    return total


def group_norm(blended, span_bits):
    total = lax.psum(jnp.sum(blended * blended).reshape(1), "dp")
    for bit in range(span_bits):
        total = total + from_partner(total, "col", bit)
    return total[0]


def local(grads, momentum, weight, max_logits, threshold):
    replicas = lax.axis_size("dp")
    span = lax.axis_size("col") // LAYERS
    span_bits = span.bit_length() - 1
    mean_grad = (
        lax.psum_scatter(grads[0].astype(jnp.float32), "dp", scatter_dimension=0, tiled=True)
        / replicas
    )
    new_momentum = momentum_rate * momentum + mean_grad
    blended = mean_grad + momentum_rate * new_momentum
    peak_all = lax.pmax(max_logits[0], "dp")
    col_index = lax.axis_index("col")
    layer = col_index // span
    layer_table = jnp.arange(LAYERS, dtype=jnp.int32)
    peak = jnp.sum(jnp.where(layer_table[:, None] == layer, peak_all, 0), axis=0)
    square_total = group_norm(blended, span_bits)
    ortho = blended / (jnp.sqrt(square_total) + epsilon)
    gram_now = group_gram(ortho, span_bits)
    blend_rms = jnp.sqrt(square_total / (F * R)).reshape(1)
    for iteration in range(ITERS):
        if iteration > 0:
            gram_now = group_gram(ortho, span_bits)
        poly_mat = coef_two * gram_now + coef_three * product(gram_now, gram_now)
        ortho = coef_one * ortho + product(ortho, poly_mat)
    update = ortho * (0.2 * jnp.sqrt(jnp.float32(max(F, R))))
    stepped = weight * (1.0 - learn_rate * decay_rate) - learn_rate * update
    row_count = ortho.shape[0]
    first_row = (col_index * replicas + lax.axis_index("dp")) * row_count
    row_ids = (first_row + jnp.arange(row_count, dtype=jnp.int32)) % F
    head_ids = row_ids // (NOPE + VDIM)
    key_rows = row_ids % (NOPE + VDIM) < NOPE
    gamma = jnp.minimum(1.0, threshold[0].astype(jnp.float32) / peak.astype(jnp.float32))
    root_gamma = jnp.sqrt(gamma)
    head_table = jnp.arange(HEADS, dtype=jnp.int32)
    per_row = jnp.sum(
        jnp.where(head_ids[:, None] == head_table[None, :], root_gamma[None, :], jnp.float32(0.0)),
        axis=1,
    )
    factor = jnp.where(key_rows, per_row, jnp.float32(1.0))
    new_master = stepped * factor[:, None]
    new_weight = lax.all_gather(new_master.astype(jnp.bfloat16), "dp", axis=0, tiled=True)
    return (new_master, new_momentum, new_weight, blend_rms)


def solution(mesh):
    return jax.shard_map(
        local,
        mesh=mesh,
        in_specs=(
            P("dp", "col", None),
            P(("col", "dp"), None),
            P(("col", "dp"), None),
            P("dp", None, None),
            P(),
        ),
        out_specs=(P(("col", "dp"), None), P(("col", "dp"), None), P("col", None), P("col")),
        check_vma=False,
    )
```

profile of v0, /device:TPU:1, one launch (start us, length us, event | category | flops | bytes accessed | tf_op | source)
XLA Modules:
  0.0 1325.8 jit_solution(7997156719461025626)
XLA Ops:
  7.2 6.6 bitcast_convert_fusion
  13.9 228.8 %reduce-scatter.2.cloned.1.call-done = f32[128,512]{1,0:T(8,128)} async-done(((f32[4096,512]{1,0:T(8,128)}), f32[128,512]{1,0:T(8,128)}) %reduce-scatter.2.cloned.1.call-update) | async-done | bytes 262160 | tf_op jit(solution)/shard_map/reduce_scatter | solution.py:53
  242.7 1.6 multiply_reduce_fusion
  244.3 59.4 %psum.42 = f32[1]{0:T(128)} all-reduce(f32[1]{0:T(128)} %bitcast.1), channel_id=1, replica_groups=mesh['dp'=32,'col'=8] {'dp'}, use_global_device_ids=true, to_apply=%region_2.3 | all-reduce | flops 1 | bytes 8 | tf_op jit(solution)/shard_map/psum | solution.py:42
  303.7 18.3 %collective-permute-start = (f32[1]{0:T(128)}, f32[1]{0:T(128)}, u32[]{:S(2)}, u32[]{:S(2)}) collective-permute-start(f32[1]{0:T(128)} %psum.42), channel_id=1, source_target_pairs={{0,1},{1,0},{2,3},{3,2},{4,5},{5,4},{6,7},{7,6},{8,9},{9,8},{10,11... | collective-permute-start | bytes 20 | tf_op jit(solution)/shard_map/ppermute | solution.py:27
  324.2 2.0 collective-permute-start.1
  327.3 3.1 fusion.28
  330.5 143.1 %all-reduce.6.cloned.1.call-done = f32[512,512]{1,0:T(8,128)} async-done(((f32[512,512]{1,0:T(8,128)}), f32[512,512]{1,0:T(8,128)}) %all-reduce.6.cloned.1.call-update) | async-done | bytes 1048592 | tf_op jit(solution)/shard_map/psum | solution.py:35
  473.5 5.3 collective-permute-start.2
  478.8 2.5 collective-permute-done.2
  481.3 1.4 add.141
  482.7 1.3 collective-permute-start.3
  484.0 23.2 %collective-permute-done.3 = f32[512,512]{1,0:T(8,128)S(1)} collective-permute-done((f32[512,512]{1,0:T(8,128)S(1)}, f32[512,512]{1,0:T(8,128)S(1)}, u32[]{:S(2)}, u32[]{:S(2)}) %collective-permute-start.3) | collective-permute-done | bytes 1048608 | tf_op jit(solution)/shard_map/ppermute | solution.py:27
  507.2 1.9 convolution_multiply_fusion.4
  510.0 2.0 fusion.36
  512.1 142.8 %all-reduce.8.cloned.1.call-done = f32[512,512]{1,0:T(8,128)} async-done(((f32[512,512]{1,0:T(8,128)}), f32[512,512]{1,0:T(8,128)}) %all-reduce.8.cloned.1.call-update) | async-done | bytes 1048592 | tf_op jit(solution)/shard_map/psum | solution.py:35
  654.8 5.3 collective-permute-start.4
  660.1 2.5 collective-permute-done.4
  662.6 1.4 add.145
  664.0 1.5 collective-permute-start.5
  665.5 23.2 %collective-permute-done.5 = f32[512,512]{1,0:T(8,128)S(1)} collective-permute-done((f32[512,512]{1,0:T(8,128)S(1)}, f32[512,512]{1,0:T(8,128)S(1)}, u32[]{:S(2)}, u32[]{:S(2)}) %collective-permute-start.5) | collective-permute-done | bytes 1048608 | tf_op jit(solution)/shard_map/ppermute | solution.py:27
  688.7 1.9 convolution_multiply_fusion.3
  691.4 2.0 fusion.37
  693.5 142.8 %all-reduce.10.cloned.1.call-done = f32[512,512]{1,0:T(8,128)} async-done(((f32[512,512]{1,0:T(8,128)}), f32[512,512]{1,0:T(8,128)}) %all-reduce.10.cloned.1.call-update) | async-done | bytes 1048592 | tf_op jit(solution)/shard_map/psum | solution.py:35
  836.2 5.3 collective-permute-start.6
  841.5 2.5 collective-permute-done.6
  844.0 1.4 add.149
  846.7 23.2 %collective-permute-done.7 = f32[512,512]{1,0:T(8,128)S(1)} collective-permute-done((f32[512,512]{1,0:T(8,128)S(1)}, f32[512,512]{1,0:T(8,128)S(1)}, u32[]{:S(2)}, u32[]{:S(2)}) %collective-permute-start.7) | collective-permute-done | bytes 1048608 | tf_op jit(solution)/shard_map/ppermute | solution.py:27
  869.9 1.9 convolution_multiply_fusion.2
  872.6 2.0 fusion.38
  874.7 142.8 %all-reduce.12.cloned.1.call-done = f32[512,512]{1,0:T(8,128)} async-done(((f32[512,512]{1,0:T(8,128)}), f32[512,512]{1,0:T(8,128)}) %all-reduce.12.cloned.1.call-update) | async-done | bytes 1048592 | tf_op jit(solution)/shard_map/psum | solution.py:35
  1017.5 5.3 collective-permute-start.8
  1022.7 2.5 collective-permute-done.8
  1025.2 1.4 add.153
  1026.7 1.5 collective-permute-start.9
  1028.2 23.2 %collective-permute-done.9 = f32[512,512]{1,0:T(8,128)S(1)} collective-permute-done((f32[512,512]{1,0:T(8,128)S(1)}, f32[512,512]{1,0:T(8,128)S(1)}, u32[]{:S(2)}, u32[]{:S(2)}) %collective-permute-start.9) | collective-permute-done | bytes 1048608 | tf_op jit(solution)/shard_map/ppermute | solution.py:27
  1051.4 1.9 convolution_multiply_fusion.1
  1054.1 2.0 fusion.39
  1056.2 142.8 %all-reduce.14.cloned.1.call-done = f32[512,512]{1,0:T(8,128)} async-done(((f32[512,512]{1,0:T(8,128)}), f32[512,512]{1,0:T(8,128)}) %all-reduce.14.cloned.1.call-update) | async-done | bytes 1048592 | tf_op jit(solution)/shard_map/psum | solution.py:35
  1198.9 5.3 collective-permute-start.10
  1204.2 2.5 collective-permute-done.10
  1206.7 1.4 add.157
  1210.1 14.1 %pmax.7 = s32[2,64]{1,0:T(2,128)S(1)} all-reduce(s32[2,64]{1,0:T(2,128)S(1)} %bitcast.19), channel_id=1, replica_groups=mesh['dp'=32,'col'=8] {'dp'}, use_global_device_ids=true, to_apply=%region_8.9 | all-reduce | flops 128 | bytes 1024 | tf_op jit(solution)/shard_map/pmax | solution.py:58
  1224.4 8.2 collective-permute-done.11
  1232.6 1.9 convolution_multiply_fusion
  1234.5 1.6 fusion.35
  1236.2 77.2 %all-gather.2.cloned.1.call-done = bf16[4096,512]{1,0:T(8,128)(2,1)} async-done(((bf16[128,512]{1,0:T(8,128)(2,1)}), bf16[4096,512]{1,0:T(8,128)(2,1)}) %all-gather.2.cloned.1.call-update) | async-done | bytes 4194320 | tf_op jit(solution)/shard_map/all_gather | solution.py:88
  1313.4 4.5 copy.16
  (38 shorter events, 8.1 us)
Async XLA Ops:
  7.2 235.5 %reduce-scatter.2.cloned.1.call-start = ((), (), s32[]{:S(2)}) async-start(), calls=%async_computation.1 | async-start | bytes 8650752 | tf_op jit(solution)/shard_map/reduce_scatter | solution.py:53
  13.8 228.8 %copy-start.3 = (f32[128,512]{1,0:T(8,128)S(1)}, f32[128,512]{1,0:T(8,128)}, u32[]{:S(2)}) copy-start(f32[128,512]{1,0:T(8,128)} %param.6) | copy-start | bytes 786436
  13.9 459.7 %all-reduce.6.cloned.1.call-start = ((), (), s32[]{:S(2)}) async-start(), calls=%async_computation.2 | async-start | bytes 2097152 | tf_op jit(solution)/shard_map/psum | solution.py:35
  244.3 264.8 %copy-start = (f32[128,512]{1,0:T(8,128)}, f32[128,512]{1,0:T(8,128)S(1)}, u32[]{:S(2)}) copy-start(f32[128,512]{1,0:T(8,128)S(1)} %get-tuple-element.13) | copy-start | bytes 786436
  303.7 19.4 %collective-permute-start = (f32[1]{0:T(128)}, f32[1]{0:T(128)}, u32[]{:S(2)}, u32[]{:S(2)}) collective-permute-start(f32[1]{0:T(128)} %psum.42), channel_id=1, source_target_pairs={{0,1},{1,0},{2,3},{3,2},{4,5},{5,4},{6,7},{7,6},{8,9},{9,8},{10,11... | collective-permute-start | bytes 20 | tf_op jit(solution)/shard_map/ppermute | solution.py:27
  324.2 2.4 collective-permute-start.1
  327.3 181.8 %copy-start.1 = (f32[128,512]{1,0:T(8,128)S(1)}, f32[128,512]{1,0:T(8,128)}, u32[]{:S(2)}) copy-start(f32[128,512]{1,0:T(8,128)} %reduce-scatter.2.cloned.1.call-done) | copy-start | bytes 786436
  330.4 324.4 %all-reduce.8.cloned.1.call-start = ((), (), s32[]{:S(2)}) async-start(), calls=%async_computation.3 | async-start | bytes 2097152 | tf_op jit(solution)/shard_map/psum | solution.py:35
  473.5 7.8 collective-permute-start.2
  482.7 24.5 %collective-permute-start.3 = (f32[512,512]{1,0:T(8,128)S(1)}, f32[512,512]{1,0:T(8,128)S(1)}, u32[]{:S(2)}, u32[]{:S(2)}) collective-permute-start(f32[512,512]{1,0:T(8,128)S(1)} %add.141), channel_id=1, source_target_pairs={{0,2},{1,3},{2,0},{3,1},{4,6},{5,7},{6,4},{7,5},{8,10},{9,11},{10,... | collective-permute-start | bytes 3145736 | tf_op jit(solution)/shard_map/ppermute | solution.py:27
  512.0 324.2 %all-reduce.10.cloned.1.call-start = ((), (), s32[]{:S(2)}) async-start(), calls=%async_computation.4 | async-start | bytes 2097152 | tf_op jit(solution)/shard_map/psum | solution.py:35
  654.8 7.8 collective-permute-start.4
  664.0 24.6 %collective-permute-start.5 = (f32[512,512]{1,0:T(8,128)S(1)}, f32[512,512]{1,0:T(8,128)S(1)}, u32[]{:S(2)}, u32[]{:S(2)}) collective-permute-start(f32[512,512]{1,0:T(8,128)S(1)} %add.145), channel_id=1, source_target_pairs={{0,2},{1,3},{2,0},{3,1},{4,6},{5,7},{6,4},{7,5},{8,10},{9,11},{10,... | collective-permute-start | bytes 3145736 | tf_op jit(solution)/shard_map/ppermute | solution.py:27
  693.4 324.1 %all-reduce.12.cloned.1.call-start = ((), (), s32[]{:S(2)}) async-start(), calls=%async_computation.5 | async-start | bytes 2097152 | tf_op jit(solution)/shard_map/psum | solution.py:35
  836.2 7.8 collective-permute-start.6
  845.4 24.5 %collective-permute-start.7 = (f32[512,512]{1,0:T(8,128)S(1)}, f32[512,512]{1,0:T(8,128)S(1)}, u32[]{:S(2)}, u32[]{:S(2)}) collective-permute-start(f32[512,512]{1,0:T(8,128)S(1)} %add.149), channel_id=1, source_target_pairs={{0,2},{1,3},{2,0},{3,1},{4,6},{5,7},{6,4},{7,5},{8,10},{9,11},{10,... | collective-permute-start | bytes 3145736 | tf_op jit(solution)/shard_map/ppermute | solution.py:27
  874.6 324.3 %all-reduce.14.cloned.1.call-start = ((), (), s32[]{:S(2)}) async-start(), calls=%async_computation.6 | async-start | bytes 2097152 | tf_op jit(solution)/shard_map/psum | solution.py:35
  1017.5 7.8 collective-permute-start.8
  1026.7 24.7 %collective-permute-start.9 = (f32[512,512]{1,0:T(8,128)S(1)}, f32[512,512]{1,0:T(8,128)S(1)}, u32[]{:S(2)}, u32[]{:S(2)}) collective-permute-start(f32[512,512]{1,0:T(8,128)S(1)} %add.153), channel_id=1, source_target_pairs={{0,2},{1,3},{2,0},{3,1},{4,6},{5,7},{6,4},{7,5},{8,10},{9,11},{10,... | collective-permute-start | bytes 3145736 | tf_op jit(solution)/shard_map/ppermute | solution.py:27
  1053.3 156.8 %copy-start.4 = (s32[1,2,64]{2,1,0:T(2,128)S(1)}, s32[1,2,64]{2,1,0:T(2,128)}, u32[]{:S(2)}) copy-start(s32[1,2,64]{2,1,0:T(2,128)} %param.8) | copy-start | bytes 1540
  1054.1 180.4 %copy-start.2 = (f32[128,512]{1,0:T(8,128)S(1)}, f32[128,512]{1,0:T(8,128)}, u32[]{:S(2)}) copy-start(f32[128,512]{1,0:T(8,128)} %param.7) | copy-start | bytes 786436
  1056.1 257.2 %all-gather.2.cloned.1.call-start = ((), (), s32[]{:S(2)}) async-start(), calls=%async_computation.7 | async-start | bytes 4325376 | tf_op jit(solution)/shard_map/all_gather | solution.py:88
  1198.9 7.8 collective-permute-start.10
  1208.1 24.5 %collective-permute-start.11 = (f32[512,512]{1,0:T(8,128)S(1)}, f32[512,512]{1,0:T(8,128)S(1)}, u32[]{:S(2)}, u32[]{:S(2)}) collective-permute-start(f32[512,512]{1,0:T(8,128)S(1)} %add.157), channel_id=1, source_target_pairs={{0,2},{1,3},{2,0},{3,1},{4,6},{5,7},{6,4},{7,5},{8,10},{9,11},{10,... | collective-permute-start | bytes 3145736 | tf_op jit(solution)/shard_map/ppermute | solution.py:27
Sparse Core Ops, SparseCore 0:
  14.0 228.6 reduce-scatter.1
  330.5 142.9 all-reduce.5
  512.1 142.6 all-reduce.7
  693.5 142.6 all-reduce.9
  874.8 142.6 all-reduce.11
  1056.3 142.6 all-reduce.13
  1236.3 77.0 all-gather.1
where the time goes:
time: 1330 us
  waiting for transfers between devices  1130 us (85%)
  blocking collectives  73.4 us (6%)
  starting transfers between devices  53.8 us (4%)
  matrix products  25.5 us (2%)
  between operations  17.9 us (1%)
  other arithmetic  15.6 us (1%)
    psum x5, waiting for transfers between devices, group_gram(): total = lax.psum(product(rows_block.T, rows_block), 'dp')  714 us
    reduce_scatter x1, waiting for transfers between devices, local(): lax.psum_scatter(grads[0].astype(jnp.float32), 'dp', scatter_dimension=0,...  229 us
    ppermute x12, waiting for transfers between devices, from_partner(): return lax.ppermute(value, axis, pairs)  115 us
    all_gather x1, waiting for transfers between devices, local(): lax.all_gather(new_master.astype(jnp.bfloat16), 'dp', axis=0, tiled=True)  77.2 us
    psum x1, blocking collectives, group_norm(): total = lax.psum(jnp.sum(blended * blended).reshape(1), 'dp')  59.4 us
    ppermute x12, starting transfers between devices, from_partner(): return lax.ppermute(value, axis, pairs)  53.5 us
  transfers between devices with their start and end apart: 19, of which 19 were waited for; matrix products, arithmetic and copies ran while one was open for 0% of the time, Pallas kernels for 0%

commit v1 on v0

--- a/solution.py
+++ b/solution.py
@@ -60,15 +60,18 @@
     layer = col_index // span
     layer_table = jnp.arange(LAYERS, dtype=jnp.int32)
     peak = jnp.sum(jnp.where(layer_table[:, None] == layer, peak_all, 0), axis=0)
-    square_total = group_norm(blended, span_bits)
-    ortho = blended / (jnp.sqrt(square_total) + epsilon)
-    gram_now = group_gram(ortho, span_bits)
+    raw_gram = group_gram(blended, span_bits)
+    square_total = jnp.sum(jnp.where(jnp.eye(R, dtype=bool), raw_gram, 0.0))
     blend_rms = jnp.sqrt(square_total / (F * R)).reshape(1)
+    inverse = 1.0 / (jnp.sqrt(square_total) + epsilon)
+    ortho = blended * inverse
+    gram_now = raw_gram * inverse * inverse
+    eye = jnp.eye(R, dtype=jnp.float32)
     for iteration in range(ITERS):
-        if iteration > 0:
-            gram_now = group_gram(ortho, span_bits)
-        poly_mat = coef_two * gram_now + coef_three * product(gram_now, gram_now)
-        ortho = coef_one * ortho + product(ortho, poly_mat)
+        factor = coef_one * eye + coef_two * gram_now + coef_three * product(gram_now, gram_now)
+        if iteration < ITERS - 1:
+            gram_now = product(product(gram_now, factor), factor)
+        ortho = product(ortho, factor)
     update = ortho * (0.2 * jnp.sqrt(jnp.float32(max(F, R))))
     stepped = weight * (1.0 - learn_rate * decay_rate) - learn_rate * update
     row_count = ortho.shape[0]

time: 1330 us -> 550 us (0.41)
  waiting for transfers between devices: 1130 us -> 463 us
  blocking collectives: 73.4 us -> 14.1 us
  starting transfers between devices: 53.8 us -> 6.68 us
    psum x5 -> x1, waiting for transfers between devices: 714 us -> 147 us  [group_gram(): total = lax.psum(product(rows_block.T, rows_block), 'dp')]
    ppermute x12 -> x2, waiting for transfers between devices: 115 us -> 10.7 us  [from_partner(): return lax.ppermute(value, axis, pairs)]
    psum x1 -> x0, blocking collectives: 59.4 us -> none  [group_norm(): total = lax.psum(jnp.sum(blended * blended).reshape(1), 'dp')]
    ppermute x12 -> x2, starting transfers between devices: 53.5 us -> 6.56 us  [from_partner(): return lax.ppermute(value, axis, pairs)]
    dot_general x15 -> x19, matrix products: 25.5 us -> 32.1 us  [product(): jnp.dot(left, right, precision=lax.Precision.HIGHEST, preferred_element_t...]
  transfers between devices with their start and end apart: 19 -> 5, of which waited for: 19 -> 5; matrix products, arithmetic and copies ran while one was open for 0% -> 0% of each run, Pallas kernels for 0% -> 0%
where the time goes in v1:
time: 550 us; the launch traced here: 548 us
  waiting for transfers between devices  463 us (84%)
  matrix products  32.1 us (6%)
  between operations  17.2 us (3%)
  blocking collectives  14.1 us (3%)
  other arithmetic  10.1 us (2%)
  starting transfers between devices  6.68 us (1%)
    reduce_scatter x1, waiting for transfers between devices, local(): lax.psum_scatter(grads[0].astype(jnp.float32), 'dp', scatter_dimension=0,...  229 us
    psum x1, waiting for transfers between devices, group_gram(): total = lax.psum(product(rows_block.T, rows_block), 'dp')  147 us
    all_gather x1, waiting for transfers between devices, local(): lax.all_gather(new_master.astype(jnp.bfloat16), 'dp', axis=0, tiled=True)  76.5 us
    dot_general x19, matrix products, product(): jnp.dot(left, right, precision=lax.Precision.HIGHEST, preferred_element_t...  32.1 us
    pmax x1, blocking collectives, local(): peak_all = lax.pmax(max_logits[0], 'dp')  14.1 us
  transfers between devices with their start and end apart: 5, of which 5 were waited for; matrix products, arithmetic and copies ran while one was open for 0% of the time, Pallas kernels for 0%

profile of v1, /device:TPU:1, one launch (start us, length us, event | category | flops | bytes accessed | tf_op | source)
XLA Modules:
  0.0 547.8 jit_solution(3842170226976016887)
XLA Ops:
  7.2 0.0 reduce-scatter.2.cloned.1.call-start
  7.2 6.6 %bitcast_convert_fusion = f32[4096,512]{1,0:T(8,128)} fusion(bf16[1,4096,512]{2,1,0:T(8,128)(2,1)} %param.5), kind=kLoop, calls=%fused_computation | loop fusion | flops 2097152 | bytes 12582912 | tf_op jit(solution)/shard_map/convert_element_type | solution.py:53
  13.8 0.0 reduce-scatter.2.cloned.1.call-update
  13.8 0.0 copy-start.4
  13.9 0.0 all-reduce.2.cloned.1.call-start
  13.9 228.7 %reduce-scatter.2.cloned.1.call-done = f32[128,512]{1,0:T(8,128)} async-done(((f32[4096,512]{1,0:T(8,128)}), f32[128,512]{1,0:T(8,128)}) %reduce-scatter.2.cloned.1.call-update) | async-done | bytes 262160 | tf_op jit(solution)/shard_map/reduce_scatter | solution.py:53
  242.7 0.0 copy-done.2
  242.7 1.0 multiply_add_fusion.1
  243.6 0.0 copy-start
  243.7 3.1 fusion.13
  246.8 0.0 all-reduce.2.cloned.1.call-update
  246.8 0.0 all-gather.2.cloned.1.call-start
  246.9 147.2 %all-reduce.2.cloned.1.call-done = f32[512,512]{1,0:T(8,128)} async-done(((f32[512,512]{1,0:T(8,128)}), f32[512,512]{1,0:T(8,128)}) %all-reduce.2.cloned.1.call-update) | async-done | bytes 1048592 | tf_op jit(solution)/shard_map/psum | solution.py:35
  394.1 5.3 collective-permute-start
  399.4 2.5 collective-permute-done
  401.9 1.4 add.94
  403.3 1.3 collective-permute-start.1
  405.3 0.0 copy-done.4
  405.3 14.1 %pmax.7 = s32[2,64]{1,0:T(2,128)S(1)} all-reduce(s32[2,64]{1,0:T(2,128)S(1)} %bitcast.38), channel_id=1, replica_groups=mesh['dp'=32,'col'=8] {'dp'}, use_global_device_ids=true, to_apply=%region_3.4 | all-reduce | flops 128 | bytes 1024 | tf_op jit(solution)/shard_map/pmax | solution.py:58
  419.4 0.1 select_reduce_fusion.2
  419.5 0.1 select_reduce_fusion.1
  419.6 8.2 %collective-permute-done.1 = f32[512,512]{1,0:T(8,128)S(1)} collective-permute-done((f32[512,512]{1,0:T(8,128)S(1)}, f32[512,512]{1,0:T(8,128)S(1)}, u32[]{:S(2)}, u32[]{:S(2)}) %collective-permute-start.1) | collective-permute-done | bytes 1048608 | tf_op jit(solution)/shard_map/ppermute | solution.py:27
  427.8 0.8 select_reduce_fusion
  429.3 2.0 fusion.6
  431.3 1.9 fusion.7
  433.2 1.8 fusion.20
  435.1 0.0 copy-start.1
  435.1 1.9 fusion.3
  437.0 1.8 fusion.22
  438.9 1.8 fusion.23
  440.7 0.0 copy-done
  440.7 0.0 copy-done.1
  440.7 0.7 fusion.10
  441.5 0.9 fusion.21
  442.4 1.9 fusion.2
  444.3 1.8 fusion.25
  446.2 1.8 fusion.26
  448.0 0.7 fusion.24
  448.8 1.9 fusion.1
  450.7 1.8 fusion.28
  452.5 0.0 copy-start.3
  452.5 1.8 fusion.29
  454.4 0.7 fusion.27
  455.1 1.9 fusion
  457.0 1.5 fusion.19
  458.5 0.0 all-gather.2.cloned.1.call-update
  459.2 76.5 %all-gather.2.cloned.1.call-done = bf16[4096,512]{1,0:T(8,128)(2,1)} async-done(((bf16[128,512]{1,0:T(8,128)(2,1)}), bf16[4096,512]{1,0:T(8,128)(2,1)}) %all-gather.2.cloned.1.call-update) | async-done | bytes 4194320 | tf_op jit(solution)/shard_map/all_gather | solution.py:91
  535.7 4.5 copy.12
  (6 shorter events, 0.1 us)
Async XLA Ops:
  7.2 235.5 %reduce-scatter.2.cloned.1.call-start = ((), (), s32[]{:S(2)}) async-start(), calls=%async_computation.1 | async-start | bytes 8650752 | tf_op jit(solution)/shard_map/reduce_scatter | solution.py:53
  13.8 228.8 %copy-start.2 = (f32[128,512]{1,0:T(8,128)S(1)}, f32[128,512]{1,0:T(8,128)}, u32[]{:S(2)}) copy-start(f32[128,512]{1,0:T(8,128)} %param.6) | copy-start | bytes 786436
  13.8 391.4 %copy-start.4 = (s32[1,2,64]{2,1,0:T(2,128)S(1)}, s32[1,2,64]{2,1,0:T(2,128)}, u32[]{:S(2)}) copy-start(s32[1,2,64]{2,1,0:T(2,128)} %param.8) | copy-start | bytes 1540
  13.9 380.2 %all-reduce.2.cloned.1.call-start = ((), (), s32[]{:S(2)}) async-start(), calls=%async_computation.2 | async-start | bytes 2097152 | tf_op jit(solution)/shard_map/psum | solution.py:35
  243.6 197.1 %copy-start = (f32[128,512]{1,0:T(8,128)}, f32[128,512]{1,0:T(8,128)S(1)}, u32[]{:S(2)}) copy-start(f32[128,512]{1,0:T(8,128)S(1)} %multiply_add_fusion.1) | copy-start | bytes 786436
  246.8 288.9 %all-gather.2.cloned.1.call-start = ((), (), s32[]{:S(2)}) async-start(), calls=%async_computation.3 | async-start | bytes 4325376 | tf_op jit(solution)/shard_map/all_gather | solution.py:91
  394.1 7.8 %collective-permute-start = (f32[512,512]{1,0:T(8,128)}, f32[512,512]{1,0:T(8,128)S(1)}, u32[]{:S(2)}, u32[]{:S(2)}) collective-permute-start(f32[512,512]{1,0:T(8,128)} %all-reduce.2.cloned.1.call-done), channel_id=1, source_target_pairs={{0,1},{1,0},{2,3},{3,2},{4,5},{5,4},{6,7},{7,6},{8,9},{9,8},{10,11... | collective-permute-start | bytes 3145736 | tf_op jit(solution)/shard_map/ppermute | solution.py:27
  403.3 24.5 %collective-permute-start.1 = (f32[512,512]{1,0:T(8,128)S(1)}, f32[512,512]{1,0:T(8,128)S(1)}, u32[]{:S(2)}, u32[]{:S(2)}) collective-permute-start(f32[512,512]{1,0:T(8,128)S(1)} %add.94), channel_id=1, source_target_pairs={{0,2},{1,3},{2,0},{3,1},{4,6},{5,7},{6,4},{7,5},{8,10},{9,11},{10,... | collective-permute-start | bytes 3145736 | tf_op jit(solution)/shard_map/ppermute | solution.py:27
  435.1 5.6 %copy-start.1 = (f32[128,512]{1,0:T(8,128)S(1)}, f32[128,512]{1,0:T(8,128)}, u32[]{:S(2)}) copy-start(f32[128,512]{1,0:T(8,128)} %reduce-scatter.2.cloned.1.call-done) | copy-start | bytes 786436
  452.5 4.5 copy-start.3
Sparse Core Ops, SparseCore 0:
  14.0 228.6 reduce-scatter.1
  247.1 147.0 all-reduce.1
  458.6 77.0 all-gather.1

commit v2 on v0

v2 whole, which is shorter than its diff:
```python
import functools

import jax
import jax.numpy as jnp
from jax import lax
from jax.experimental import pallas as pl
from jax.experimental.pallas import tpu as pltpu
from jax.sharding import PartitionSpec as P

R = 512
HEADS = 64
NOPE = 128
VDIM = 128
ITERS = 5
LAYERS = 2
F = 16384

NZ = 8
NX = 4
NY = 4
BLOCK = 128
CUT = 80

momentum_rate = 0.95
epsilon = 1e-07
coef_one = 3.4445
coef_two = -4.775
coef_three = 2.0315
learn_rate = 0.02
decay_rate = 0.1

ORDER = (4, -3, 3, -2, 2, -1, 1, 0)
PAIRS = [(i, j) for i in range(4) for j in range(i, 4)]
HALF = len(PAIRS) * BLOCK // 2
PART = HALF // 8
SLAB = PART // 8


def exact(left, right, dims=((1,), (0,))):
    return lax.dot_general(
        left,
        right,
        (dims, ((), ())),
        precision=lax.Precision.HIGHEST,
        preferred_element_type=jnp.float32,
    )


def kernel(
    grads,
    momentum,
    weight,
    max_logits,
    threshold,
    new_master,
    new_momentum,
    new_weight,
    blend_rms,
    own,
    rx,
    relay,
    zs,
    zr,
    packed,
    core_in,
    half_sum,
    xy_in,
    slab_out,
    slab_in,
    slab_sum,
    slab_all,
    full,
    gram,
    factor_mat,
    ortho,
    rounded,
    ml_out,
    ml_x,
    ml_mid,
    ml_z,
    s_local,
    s_x,
    r_x,
    s_z,
    r_z,
    s_ml,
    r_ml,
    s_g,
    r_g,
    s_az,
    r_az,
    s_ax,
    r_ax,
    s_bx,
    r_bx,
    s_bz,
    r_bz,
):
    d = lax.axis_index("dp")
    c = lax.axis_index("col")
    z, x = d // NX, d % NX
    y, core = c // 2, c % 2
    ybase = (y // 2) * 2
    xr, xl, xo = (x + 1) % NX, (x + 3) % NX, (x + 2) % NX
    zup, zdn = (z + 1) % NZ, (z + NZ - 1) % NZ
    m8 = x * 2 + y % 2

    def at_x(xx):
        return (z * NX + xx, c)

    def at_z(zz):
        return (zz * NX + x, c)

    def at_xy(p):
        return (z * NX + p // 2, (ybase + p % 2) * 2 + core)

    partner = (d, y * 2 + 1 - core)

    def send(src, dst, ss, rs, to):
        copy = pltpu.make_async_remote_copy(
            src_ref=src,
            dst_ref=dst,
            send_sem=ss,
            recv_sem=rs,
            device_id=to,
            device_id_type=pl.DeviceIdType.MESH,
        )
        copy.start()
        return copy

    sent = []

    ml_out[...] = jnp.zeros_like(ml_out)
    ml_out[0:2, 0:HEADS] = max_logits[0]

    barrier = pltpu.get_barrier_semaphore()
    mates = [at_xy((m8 + r) % 8) for r in range(1, 8)]
    mates += [at_z((z + r) % NZ) for r in range(1, NZ)]
    mates += [partner]
    for mate in mates:
        pl.semaphore_signal(
            barrier, inc=1, device_id=mate, device_id_type=pl.DeviceIdType.MESH
        )
    own_copy = pltpu.make_async_copy(grads.at[:, x], own, s_local.at[0])
    own_copy.start()
    pl.semaphore_wait(barrier, len(mates))

    chunks = {}
    forwards = {}

    def start_chunk(j):
        zt = (z + ORDER[j] + NZ) % NZ
        chunks[j] = [
            send(grads.at[zt, xo, 0:64], relay.at[j, 0], s_x.at[j, 2], r_x.at[j, 2], at_x(xr)),
            send(grads.at[zt, xo, 64:128], relay.at[j, 1], s_x.at[j, 3], r_x.at[j, 3], at_x(xl)),
            send(grads.at[zt, xr], rx.at[j, 0], s_x.at[j, 0], r_x.at[j, 0], at_x(xr)),
            send(grads.at[zt, xl], rx.at[j, 1], s_x.at[j, 1], r_x.at[j, 1], at_x(xl)),
        ]
        sent.extend(chunks[j])

    def forward_chunk(j):
        chunks[j][0].wait_recv()
        one = send(relay.at[j, 0], rx.at[j, 2, 0:64], s_x.at[j, 4], r_x.at[j, 4], at_x(xr))
        chunks[j][1].wait_recv()
        two = send(relay.at[j, 1], rx.at[j, 2, 64:128], s_x.at[j, 5], r_x.at[j, 5], at_x(xl))
        forwards[j] = [one, two]
        sent.extend(forwards[j])

    ring = {}

    def finish_chunk(j):
        offset = ORDER[j]
        zt = (z + offset + NZ) % NZ
        chunks[j][2].wait_recv()
        chunks[j][3].wait_recv()
        forwards[j][0].wait_recv()
        forwards[j][1].wait_recv()
        value = own[zt].astype(jnp.float32) + rx[j, 0].astype(jnp.float32)
        value = value + (rx[j, 1].astype(jnp.float32) + rx[j, 2].astype(jnp.float32))
        if offset == 4:
            zs[0, 0, 0:64] = value[0:64]
            zs[1, 0, 0:64] = value[64:128]
            for way, to in ((0, zdn), (1, zup)):
                ring[way, 0] = send(
                    zs.at[way, 0, 0:64], zr.at[way, 0, 0:64], s_z.at[way, 0], r_z.at[way, 0], at_z(to)
                )
                sent.append(ring[way, 0])
        elif offset != 0:
            way = 0 if offset < 0 else 1
            to = zdn if offset < 0 else zup
            step = 4 - abs(offset)
            ring[way, step - 1].wait_recv()
            if step == 1:
                part = zr[way, 0, 0:64]
                low = value[0:64] + part if way == 0 else value[0:64]
                high = value[64:128] if way == 0 else value[64:128] + part
                zs[way, 1, 0:64] = low
                zs[way, 1, 64:128] = high
            else:
                zs[way, step] = value + zr[way, step - 1]
            ring[way, step] = send(
                zs.at[way, step], zr.at[way, step], s_z.at[way, step], r_z.at[way, step], at_z(to)
            )
            sent.append(ring[way, step])
        else:
            ring[0, 3].wait_recv()
            ring[1, 3].wait_recv()
            return value + (zr[0, 3] + zr[1, 3])

    start_chunk(0)
    start_chunk(1)
    ml_sends = []
    for r in range(1, NX):
        ml_sends.append(
            send(ml_out, ml_x.at[r - 1], s_ml.at[r - 1], r_ml.at[r - 1], at_x((x + r) % NX))
        )
    sent.extend(ml_sends)
    total = None
    for j in range(8):
        forward_chunk(j)
        if j + 2 < 8:
            start_chunk(j + 2)
        if j == 0:
            own_copy.wait()
        else:
            finish_chunk(j - 1)
        if j == 2:
            for copy in ml_sends:
                copy.wait_recv()
            ml_mid[...] = jnp.maximum(
                jnp.maximum(ml_out[...], ml_x[0]), jnp.maximum(ml_x[1], ml_x[2])
            )
            ml_sends = []
            for r in range(1, NZ):
                ml_sends.append(
                    send(ml_mid, ml_z.at[r - 1], s_ml.at[r + 2], r_ml.at[r + 2], at_z((z + r) % NZ))
                )
            sent.extend(ml_sends)
    total = finish_chunk(7)

    mean_grad = total * (1.0 / (NZ * NX))
    moment = momentum_rate * momentum[...] + mean_grad
    new_momentum[...] = moment
    blended = mean_grad + momentum_rate * moment
    ortho[...] = blended

    low = 0
    for i in range(4):
        strip = exact(ortho[:, i * BLOCK : (i + 1) * BLOCK], ortho[:, i * BLOCK :], ((0,), (0,)))
        for j in range(i, 4):
            packed[low * BLOCK : (low + 1) * BLOCK] = strip[:, (j - i) * BLOCK : (j - i + 1) * BLOCK]
            low += 1
    theirs = pl.ds(pl.multiple_of((1 - core) * HALF, BLOCK // 2), HALF)
    mine = pl.ds(pl.multiple_of(core * HALF, BLOCK // 2), HALF)
    copy = send(packed.at[theirs], core_in, s_g.at[0], r_g.at[0], partner)
    sent.append(copy)
    copy.wait_recv()
    half_sum[...] = packed[mine] + core_in[...]

    copies = []
    for r in range(1, 8):
        p = (m8 + r) % 8
        piece = pl.ds(pl.multiple_of(p * PART, 8), PART)
        copies.append(send(half_sum.at[piece], xy_in.at[r - 1], s_g.at[r], r_g.at[r], at_xy(p)))
    sent.extend(copies)
    my_piece = pl.ds(pl.multiple_of(m8 * PART, 8), PART)
    part = half_sum[my_piece]
    for r in range(1, 8):
        copies[r - 1].wait_recv()
        part = part + xy_in[r - 1]
    for i in range(8):
        slab_out[i] = part[i * SLAB : (i + 1) * SLAB]
    copies = []
    for r in range(1, NZ):
        zt = (z + r) % NZ
        copies.append(
            send(slab_out.at[zt], slab_in.at[r - 1], s_g.at[7 + r], r_g.at[7 + r], at_z(zt))
        )
    sent.extend(copies)
    slab = slab_out[z]
    for r in range(1, NZ):
        copies[r - 1].wait_recv()
        slab = slab + slab_in[r - 1]
    slab_sum[...] = slab
    slab_all[z] = slab
    copies = []
    for r in range(1, NZ):
        zt = (z + r) % NZ
        copies.append(
            send(slab_sum, slab_all.at[z], s_g.at[14 + r], r_g.at[14 + r], at_z(zt))
        )
    sent.extend(copies)
    for copy in copies:
        copy.wait_recv()
    here = pl.ds(pl.multiple_of(core * HALF + m8 * PART, 8), PART)
    full[here] = jnp.concatenate([slab_all[i] for i in range(8)], axis=0)
    copies = []
    for r in range(1, 8):
        p = (m8 + r) % 8
        copies.append(send(full.at[here], full.at[here], s_g.at[21 + r], r_g.at[21 + r], at_xy(p)))
    sent.extend(copies)
    for copy in copies:
        copy.wait_recv()
    copy = send(full.at[mine], full.at[mine], s_g.at[29], r_g.at[29], partner)
    sent.append(copy)
    copy.wait_recv()

    rows = lax.broadcasted_iota(jnp.int32, (BLOCK, BLOCK), 0)
    cols = lax.broadcasted_iota(jnp.int32, (BLOCK, BLOCK), 1)
    diagonal = jnp.zeros((BLOCK, BLOCK), jnp.float32)
    for low, (i, j) in enumerate(PAIRS):
        if i == j:
            block = full[low * BLOCK : (low + 1) * BLOCK]
            diagonal = diagonal + jnp.where(rows == cols, block, 0.0)
    square_total = jnp.sum(jnp.sum(diagonal, axis=0, keepdims=True), axis=1, keepdims=True)
    inverse = 1.0 / (jnp.sqrt(square_total) + epsilon)
    blend_rms[0] = jnp.sqrt(square_total * (1.0 / (F * R)))[0, 0]
    for low, (i, j) in enumerate(PAIRS):
        block = full[low * BLOCK : (low + 1) * BLOCK] * inverse * inverse
        gram[i * BLOCK : (i + 1) * BLOCK, j * BLOCK : (j + 1) * BLOCK] = block
        if i != j:
            gram[j * BLOCK : (j + 1) * BLOCK, i * BLOCK : (i + 1) * BLOCK] = block.T
    ortho[...] = ortho[...] * inverse

    def fill_factor():
        now = gram[...]
        square = exact(now, now)
        row_ids = lax.broadcasted_iota(jnp.int32, (R, R), 0)
        col_ids = lax.broadcasted_iota(jnp.int32, (R, R), 1)
        factor_mat[...] = (
            jnp.where(row_ids == col_ids, coef_one, 0.0) + coef_two * now + coef_three * square
        )

    def step(k, carry):
        fill_factor()
        gram[...] = exact(gram[...], factor_mat[...])
        gram[...] = exact(gram[...], factor_mat[...])
        ortho[...] = exact(ortho[...], factor_mat[...])
        return carry

    lax.fori_loop(0, ITERS - 1, step, 0)
    fill_factor()
    last = exact(ortho[...], factor_mat[...])

    for copy in ml_sends:
        copy.wait_recv()
    peaks = ml_mid[...]
    for r in range(NZ - 1):
        peaks = jnp.maximum(peaks, ml_z[r])
    head = (c % (2 * NY // LAYERS)) * (HEADS * LAYERS // (2 * NY)) + d // 2
    layer = c // (2 * NY // LAYERS)
    rows = lax.broadcasted_iota(jnp.int32, (8, 128), 0)
    cols = lax.broadcasted_iota(jnp.int32, (8, 128), 1)
    chosen = jnp.where((rows == layer) & (cols == head), peaks, 0)
    peak = jnp.max(jnp.max(chosen, axis=0, keepdims=True), axis=1, keepdims=True)
    limit = jnp.full((1, 1), threshold[0], jnp.int32).astype(jnp.float32)
    gamma = jnp.minimum(1.0, limit / peak.astype(jnp.float32))
    scale = jnp.where(jnp.full((1, 1), d % 2, jnp.int32) == 0, jnp.sqrt(gamma), 1.0)
    update = last * (0.2 * float(max(F, R)) ** 0.5)
    stepped = weight[...] * (1.0 - learn_rate * decay_rate) - learn_rate * update
    master = stepped * scale
    new_master[...] = master
    rounded[...] = master.astype(jnp.bfloat16)

    local_copy = pltpu.make_async_copy(rounded, new_weight.at[z, x], s_local.at[1])
    local_copy.start()
    bx = [
        send(rounded.at[CUT:BLOCK], new_weight.at[z, x, CUT:BLOCK], s_bx.at[0], r_bx.at[0], at_x(xr)),
        send(rounded.at[CUT:BLOCK], new_weight.at[z, x, CUT:BLOCK], s_bx.at[1], r_bx.at[1], at_x(xl)),
    ]
    az = {}
    az[0, 0] = send(rounded.at[0:CUT], new_weight.at[z, x, 0:CUT], s_az.at[0, 0], r_az.at[0, 0], at_z(zup))
    az[1, 0] = send(rounded.at[0:CUT], new_weight.at[z, x, 0:CUT], s_az.at[1, 0], r_az.at[1, 0], at_z(zdn))

    ax = {}

    def spread(slot, zz, src):
        ax[slot] = [
            send(src, new_weight.at[zz, x, 0:CUT], s_ax.at[slot, 0], r_ax.at[slot, 0], at_x(xr)),
            send(src, new_weight.at[zz, x, 0:CUT], s_ax.at[slot, 1], r_ax.at[slot, 1], at_x(xl)),
        ]
        sent.extend(ax[slot])

    def spread_on(slot, zz):
        ax[slot][0].wait_recv()
        left = new_weight.at[zz, xl, 0:48]
        one = send(left, left, s_ax.at[slot, 2], r_ax.at[slot, 2], at_x(xr))
        ax[slot][1].wait_recv()
        right = new_weight.at[zz, xr, 48:CUT]
        two = send(right, right, s_ax.at[slot, 3], r_ax.at[slot, 3], at_x(xl))
        ax[slot].extend([one, two])
        sent.extend([one, two])

    spread(0, z, rounded.at[0:CUT])
    bx[0].wait_recv()
    left = new_weight.at[z, xl, CUT : CUT + 32]
    bx.append(send(left, left, s_bx.at[2], r_bx.at[2], at_x(xr)))
    bx[1].wait_recv()
    right = new_weight.at[z, xr, CUT + 32 : BLOCK]
    bx.append(send(right, right, s_bx.at[3], r_bx.at[3], at_x(xl)))
    local_copy.wait()
    bx[2].wait_recv()
    bx[3].wait_recv()
    sent.extend(bx)
    bz = {}

    def ring_b(step):
        if step < 3:
            up = new_weight.at[(z + NZ - step) % NZ, :, CUT:BLOCK]
            down = new_weight.at[(z + step) % NZ, :, CUT:BLOCK]
        else:
            up = new_weight.at[(z + NZ - step) % NZ, 0:2, CUT:BLOCK]
            down = new_weight.at[(z + step) % NZ, 2:4, CUT:BLOCK]
        bz[0, step] = send(up, up, s_bz.at[0, step], r_bz.at[0, step], at_z(zup))
        bz[1, step] = send(down, down, s_bz.at[1, step], r_bz.at[1, step], at_z(zdn))
        sent.extend([bz[0, step], bz[1, step]])

    def ring_a(step):
        if step < 3:
            up = new_weight.at[(z + NZ - step) % NZ, x, 0:CUT]
            down = new_weight.at[(z + step) % NZ, x, 0:CUT]
        else:
            up = new_weight.at[(z + NZ - step) % NZ, x, 0:48]
            down = new_weight.at[(z + step) % NZ, x, 48:CUT]
        az[0, step] = send(up, up, s_az.at[0, step], r_az.at[0, step], at_z(zup))
        az[1, step] = send(down, down, s_az.at[1, step], r_az.at[1, step], at_z(zdn))

    ring_b(0)
    for step in range(1, 4):
        az[0, step - 1].wait_recv()
        az[1, step - 1].wait_recv()
        ring_a(step)
        up, down = (z + NZ - step) % NZ, (z + step) % NZ
        spread(2 * step - 1, up, new_weight.at[up, x, 0:CUT])
        spread(2 * step, down, new_weight.at[down, x, 0:CUT])
        if step == 1:
            spread_on(0, z)
        else:
            spread_on(2 * step - 3, (z + NZ - step + 1) % NZ)
            spread_on(2 * step - 2, (z + step - 1) % NZ)
        bz[0, step - 1].wait_recv()
        bz[1, step - 1].wait_recv()
        ring_b(step)
    az[0, 3].wait_recv()
    az[1, 3].wait_recv()
    far = (z + 4) % NZ
    spread(7, far, new_weight.at[far, x, 0:CUT])
    spread_on(5, (z + NZ - 3) % NZ)
    spread_on(6, (z + 3) % NZ)
    spread_on(7, far)
    bz[0, 3].wait_recv()
    bz[1, 3].wait_recv()
    for slot in range(8):
        ax[slot][2].wait_recv()
        ax[slot][3].wait_recv()
    sent.extend(az.values())
    for copy in sent:
        copy.wait_send()


def local(grads, momentum, weight, max_logits, threshold):
    vmem = pl.BlockSpec(memory_space=pltpu.VMEM)
    smem = pl.BlockSpec(memory_space=pltpu.SMEM)
    hbm = pl.BlockSpec(memory_space=pl.ANY)
    f32, bf16, i32 = jnp.float32, jnp.bfloat16, jnp.int32
    dma = pltpu.SemaphoreType.DMA
    new_master, new_momentum, new_weight, blend_rms = pl.pallas_call(
        kernel,
        out_shape=(
            jax.ShapeDtypeStruct((BLOCK, R), f32),
            jax.ShapeDtypeStruct((BLOCK, R), f32),
            jax.ShapeDtypeStruct((NZ, NX, BLOCK, R), bf16),
            jax.ShapeDtypeStruct((1,), f32),
        ),
        in_specs=[hbm, vmem, vmem, vmem, smem],
        out_specs=(vmem, vmem, hbm, smem),
        scratch_shapes=[
            pltpu.VMEM((NZ, BLOCK, R), bf16),
            pltpu.VMEM((8, 3, BLOCK, R), bf16),
            pltpu.VMEM((8, 2, BLOCK // 2, R), bf16),
            pltpu.VMEM((2, 4, BLOCK, R), f32),
            pltpu.VMEM((2, 4, BLOCK, R), f32),
            pltpu.VMEM((2 * HALF, BLOCK), f32),
            pltpu.VMEM((HALF, BLOCK), f32),
            pltpu.VMEM((HALF, BLOCK), f32),
            pltpu.VMEM((7, PART, BLOCK), f32),
            pltpu.VMEM((8, SLAB, BLOCK), f32),
            pltpu.VMEM((7, SLAB, BLOCK), f32),
            pltpu.VMEM((SLAB, BLOCK), f32),
            pltpu.VMEM((8, SLAB, BLOCK), f32),
            pltpu.VMEM((2 * HALF, BLOCK), f32),
            pltpu.VMEM((R, R), f32),
            pltpu.VMEM((R, R), f32),
            pltpu.VMEM((BLOCK, R), f32),
            pltpu.VMEM((BLOCK, R), bf16),
            pltpu.VMEM((8, 128), i32),
            pltpu.VMEM((3, 8, 128), i32),
            pltpu.VMEM((8, 128), i32),
            pltpu.VMEM((7, 8, 128), i32),
            dma((2,)),
            dma((8, 6)),
            dma((8, 6)),
            dma((2, 4)),
            dma((2, 4)),
            dma((10,)),
            dma((10,)),
            dma((30,)),
            dma((30,)),
            dma((2, 4)),
            dma((2, 4)),
            dma((8, 4)),
            dma((8, 4)),
            dma((4,)),
            dma((4,)),
            dma((2, 4)),
            dma((2, 4)),
        ],
        compiler_params=pltpu.CompilerParams(
            collective_id=0, has_side_effects=True, vmem_limit_bytes=48 * 1024 * 1024
        ),
        name="muon",
    )(grads.reshape(NZ, NX, BLOCK, R), momentum, weight, max_logits, threshold)
    return (new_master, new_momentum, new_weight.reshape(NZ * NX * BLOCK, R), blend_rms)


def solution(mesh):
    return jax.shard_map(
        local,
        mesh=mesh,
        in_specs=(
            P("dp", "col", None),
            P(("col", "dp"), None),
            P(("col", "dp"), None),
            P("dp", None, None),
            P(),
        ),
        out_specs=(P(("col", "dp"), None), P(("col", "dp"), None), P("col", None), P("col")),
        check_vma=False,
    )
```

time: 1330 us -> 158 us (0.12)
  waiting for transfers between devices: 1130 us -> 0 us
  Pallas kernels: 0 us -> 148 us
  blocking collectives: 73.4 us -> 0 us
  starting transfers between devices: 53.8 us -> 0 us
  matrix products: 25.5 us -> 0 us
  other arithmetic: 15.6 us -> 0 us
  between operations: 17.9 us -> 3.04 us
    psum x5 -> x0, waiting for transfers between devices: 714 us -> none  [group_gram(): total = lax.psum(product(rows_block.T, rows_block), 'dp')]
    reduce_scatter x1 -> x0, waiting for transfers between devices: 229 us -> none  [local(): lax.psum_scatter(grads[0].astype(jnp.float32), 'dp', scatter_dimension=0,...]
    pallas_call x0 -> x1, Pallas kernels: none -> 148 us  [local(): pl.pallas_call(kernel, out_shape=(jax.ShapeDtypeStruct((BLOCK, R), f32),...]
    ppermute x12 -> x0, waiting for transfers between devices: 115 us -> none  [from_partner(): return lax.ppermute(value, axis, pairs)]
    all_gather x1 -> x0, waiting for transfers between devices: 77.2 us -> none  [local(): lax.all_gather(new_master.astype(jnp.bfloat16), 'dp', axis=0, tiled=True)]
    psum x1 -> x0, blocking collectives: 59.4 us -> none  [group_norm(): total = lax.psum(jnp.sum(blended * blended).reshape(1), 'dp')]
    ppermute x12 -> x0, starting transfers between devices: 53.5 us -> none  [from_partner(): return lax.ppermute(value, axis, pairs)]
    dot_general x15 -> x0, matrix products: 25.5 us -> none  [product(): jnp.dot(left, right, precision=lax.Precision.HIGHEST, preferred_element_t...]
  transfers between devices with their start and end apart: 19 -> 0, of which waited for: 19 -> 0; matrix products, arithmetic and copies ran while one was open for 0% -> 0% of each run, Pallas kernels for 0% -> 0%
where the time goes in v2:
time: 158 us; the launch traced here: 157 us
  Pallas kernels  148 us (94%)
  local copies, waits for them, and re-layouts  5.99 us (4%)
  between operations  3.04 us (2%)
    pallas_call x1, Pallas kernels, local(): pl.pallas_call(kernel, out_shape=(jax.ShapeDtypeStruct((BLOCK, R), f32),...  148 us
    unnamed x9, local copies, waits for them, and re-layouts  5.99 us

profile of v2, /device:TPU:1, one launch (start us, length us, event | category | flops | bytes accessed | tf_op | source)
XLA Modules:
  0.0 156.7 jit_solution(13063115235561620106)
XLA Ops:
  1.3 0.0 copy-start
  1.3 0.9 copy-done
  2.2 0.0 copy-start.1
  2.2 0.9 copy-done.1
  3.2 0.0 copy-start.2
  3.2 0.7 copy-done.2
  3.9 147.6 %muon.1 = (f32[128,512]{1,0:T(8,128)S(1)}, f32[128,512]{1,0:T(8,128)S(1)}, bf16[8,4,128,512]{3,2,1,0:T(8,128)(2,1)S(1)}, f32[1]{0:T(128)}) custom-call(bf16[8,4,128,512]{3,2,1,0:T(8,128)(2,1)} %bitcast.3, f32[128,512]{1,0:T(8,128)S(1)} %copy-done, f32[128,512]{1,0:T(8,128)S(1)} %copy-done.1, s32[1,2,64]{2,1,0:T(2,128)S(1)} %copy-done.2, s32[1]{0:T(128)S(6)} %copy.13.threshold), custom_call_target="tpu_custom_call" | custom-call | tf_op jit(solution)/shard_map/muon/pallas_call | solution.py:467
  151.5 0.7 copy.14
  152.2 0.7 copy.15
  152.9 2.0 %copy.16 = bf16[4096,512]{1,0:T(8,128)(2,1)} copy(bf16[4096,512]{1,0:T(8,128)(2,1)S(1)} %bitcast.2) | data formatting | bytes 8388608
Async XLA Ops:
  1.3 1.0 copy-start
  2.2 0.9 copy-start.1
  3.2 0.7 copy-start.2

commit v3 on v2

--- a/solution.py
+++ b/solution.py
@@ -20,6 +20,9 @@
 NY = 4
 BLOCK = 128
 CUT = 80
+CA = 384
+CB = R - CA
+FINE = 2
 
 momentum_rate = 0.95
 epsilon = 1e-07
@@ -44,6 +47,32 @@
         precision=lax.Precision.HIGHEST,
         preferred_element_type=jnp.float32,
     )
+
+
+def halves(value, count):
+    terms = []
+    for left in range(count, 0, -1):
+        terms.append(value.astype(jnp.bfloat16))
+        if left > 1:
+            value = value - terms[-1].astype(jnp.float32)
+    return terms
+
+
+def split_product(left, right):
+    def dot(i, j):
+        return jnp.dot(left[i], right[j], preferred_element_type=jnp.float32)
+
+    total = dot(0, 1) + dot(1, 0)
+    if len(left) == 3:
+        total = total + (dot(1, 1) + (dot(0, 2) + dot(2, 0)))
+    return dot(0, 0) + total
+
+
+def mirrored(left, right):
+    half = R // 2
+    top = split_product([term[0:half] for term in left], right)
+    low = split_product([term[half:R] for term in left], [term[:, half:R] for term in right])
+    return jnp.concatenate([top, jnp.concatenate([top[:, half:R].T, low], axis=1)], axis=0)
 
 
 def kernel(
@@ -57,10 +86,19 @@
     new_weight,
     blend_rms,
     own,
+    own_b,
     rx,
-    relay,
     zs,
     zr,
+    bs,
+    br,
+    b_sum,
+    b_in,
+    moment_in,
+    weight_in,
+    moment_out,
+    master_out,
+    ml_in,
     packed,
     core_in,
     half_sum,
@@ -71,7 +109,6 @@
     slab_all,
     full,
     gram,
-    factor_mat,
     ortho,
     rounded,
     ml_out,
@@ -83,6 +120,8 @@
     r_x,
     s_z,
     r_z,
+    s_b,
+    r_b,
     s_ml,
     r_ml,
     s_g,
@@ -130,9 +169,6 @@
 
     sent = []
 
-    ml_out[...] = jnp.zeros_like(ml_out)
-    ml_out[0:2, 0:HEADS] = max_logits[0]
-
     barrier = pltpu.get_barrier_semaphore()
     mates = [at_xy((m8 + r) % 8) for r in range(1, 8)]
     mates += [at_z((z + r) % NZ) for r in range(1, NZ)]
@@ -141,40 +177,42 @@
         pl.semaphore_signal(
             barrier, inc=1, device_id=mate, device_id_type=pl.DeviceIdType.MESH
         )
-    own_copy = pltpu.make_async_copy(grads.at[:, x], own, s_local.at[0])
-    own_copy.start()
+    loads = [
+        pltpu.make_async_copy(grads.at[:, :, :, CA:R], own_b, s_local.at[0]),
+        pltpu.make_async_copy(grads.at[:, x, :, 0:CA], own, s_local.at[1]),
+        pltpu.make_async_copy(max_logits, ml_in, s_local.at[2]),
+        pltpu.make_async_copy(momentum, moment_in, s_local.at[3]),
+        pltpu.make_async_copy(weight, weight_in, s_local.at[4]),
+    ]
+    for copy in loads:
+        copy.start()
     pl.semaphore_wait(barrier, len(mates))
 
     chunks = {}
-    forwards = {}
 
     def start_chunk(j):
         zt = (z + ORDER[j] + NZ) % NZ
-        chunks[j] = [
-            send(grads.at[zt, xo, 0:64], relay.at[j, 0], s_x.at[j, 2], r_x.at[j, 2], at_x(xr)),
-            send(grads.at[zt, xo, 64:128], relay.at[j, 1], s_x.at[j, 3], r_x.at[j, 3], at_x(xl)),
-            send(grads.at[zt, xr], rx.at[j, 0], s_x.at[j, 0], r_x.at[j, 0], at_x(xr)),
-            send(grads.at[zt, xl], rx.at[j, 1], s_x.at[j, 1], r_x.at[j, 1], at_x(xl)),
-        ]
+        chunks[j] = []
+        for r in (1, 3, 2):
+            xt = (x + r) % NX
+            chunks[j].append(
+                send(
+                    grads.at[zt, xt, :, 0:CA],
+                    rx.at[j, r - 1],
+                    s_x.at[j, r - 1],
+                    r_x.at[j, r - 1],
+                    at_x(xt),
+                )
+            )
         sent.extend(chunks[j])
-
-    def forward_chunk(j):
-        chunks[j][0].wait_recv()
-        one = send(relay.at[j, 0], rx.at[j, 2, 0:64], s_x.at[j, 4], r_x.at[j, 4], at_x(xr))
-        chunks[j][1].wait_recv()
-        two = send(relay.at[j, 1], rx.at[j, 2, 64:128], s_x.at[j, 5], r_x.at[j, 5], at_x(xl))
-        forwards[j] = [one, two]
-        sent.extend(forwards[j])
 
     ring = {}
 
     def finish_chunk(j):
         offset = ORDER[j]
         zt = (z + offset + NZ) % NZ
-        chunks[j][2].wait_recv()
-        chunks[j][3].wait_recv()
-        forwards[j][0].wait_recv()
-        forwards[j][1].wait_recv()
+        for copy in chunks[j]:
+            copy.wait_recv()
         value = own[zt].astype(jnp.float32) + rx[j, 0].astype(jnp.float32)
         value = value + (rx[j, 1].astype(jnp.float32) + rx[j, 2].astype(jnp.float32))
         if offset == 4:
@@ -192,10 +230,8 @@
             ring[way, step - 1].wait_recv()
             if step == 1:
                 part = zr[way, 0, 0:64]
-                low = value[0:64] + part if way == 0 else value[0:64]
-                high = value[64:128] if way == 0 else value[64:128] + part
-                zs[way, 1, 0:64] = low
-                zs[way, 1, 64:128] = high
+                zs[way, 1, 0:64] = value[0:64] + part if way == 0 else value[0:64]
+                zs[way, 1, 64:128] = value[64:128] if way == 0 else value[64:128] + part
             else:
                 zs[way, step] = value + zr[way, step - 1]
             ring[way, step] = send(
@@ -207,24 +243,51 @@
             ring[1, 3].wait_recv()
             return value + (zr[0, 3] + zr[1, 3])
 
+    wheel = {}
+
+    def turn(step):
+        for way, to in ((0, zdn), (1, zup)):
+            sign = -1 if way == 0 else 1
+            zt = (z + sign * (4 - step) + NZ) % NZ
+            lo, up = 2 * way, 2 * way + 2
+            if step == 0:
+                bs[way, 0, lo:up] = own_b[zt, lo:up].astype(jnp.float32)
+                src, dst = bs.at[way, 0, lo:up], br.at[way, 0, lo:up]
+            else:
+                wheel[way, step - 1].wait_recv()
+                if step == 1:
+                    rest = 2 - lo
+                    bs[way, 1, lo:up] = own_b[zt, lo:up].astype(jnp.float32) + br[way, 0, lo:up]
+                    bs[way, 1, rest : rest + 2] = own_b[zt, rest : rest + 2].astype(jnp.float32)
+                else:
+                    bs[way, step] = own_b[zt].astype(jnp.float32) + br[way, step - 1]
+                src, dst = bs.at[way, step], br.at[way, step]
+            wheel[way, step] = send(src, dst, s_b.at[way, step], r_b.at[way, step], at_z(to))
+            sent.append(wheel[way, step])
+
     start_chunk(0)
     start_chunk(1)
+    loads[0].wait()
+    turn(0)
+    start_chunk(2)
+    loads[2].wait()
+    ml_out[...] = jnp.zeros_like(ml_out)
+    ml_out[0:2, 0:HEADS] = ml_in[0]
     ml_sends = []
     for r in range(1, NX):
         ml_sends.append(
             send(ml_out, ml_x.at[r - 1], s_ml.at[r - 1], r_ml.at[r - 1], at_x((x + r) % NX))
         )
     sent.extend(ml_sends)
-    total = None
-    for j in range(8):
-        forward_chunk(j)
-        if j + 2 < 8:
-            start_chunk(j + 2)
-        if j == 0:
-            own_copy.wait()
-        else:
-            finish_chunk(j - 1)
-        if j == 2:
+    loads[1].wait()
+    cross = []
+    for j in range(7):
+        finish_chunk(j)
+        if j + 3 < 8:
+            start_chunk(j + 3)
+        if j in (0, 2, 4):
+            turn(j // 2 + 1)
+        if j == 3:
             for copy in ml_sends:
                 copy.wait_recv()
             ml_mid[...] = jnp.maximum(
@@ -236,13 +299,31 @@
                     send(ml_mid, ml_z.at[r - 1], s_ml.at[r + 2], r_ml.at[r + 2], at_z((z + r) % NZ))
                 )
             sent.extend(ml_sends)
-    total = finish_chunk(7)
-
-    mean_grad = total * (1.0 / (NZ * NX))
-    moment = momentum_rate * momentum[...] + mean_grad
-    new_momentum[...] = moment
-    blended = mean_grad + momentum_rate * moment
-    ortho[...] = blended
+        if j == 5:
+            wheel[0, 3].wait_recv()
+            wheel[1, 3].wait_recv()
+            b_sum[...] = own_b[z].astype(jnp.float32) + (br[0, 3] + br[1, 3])
+            for r in range(1, NX):
+                xt = (x + r) % NX
+                cross.append(
+                    send(b_sum.at[xt], b_in.at[r - 1], s_b.at[2, r - 1], r_b.at[2, r - 1], at_x(xt))
+                )
+            sent.extend(cross)
+    total_a = finish_chunk(7)
+    loads[3].wait()
+    loads[4].wait()
+    total_b = b_sum[x]
+    for r in range(1, NX):
+        cross[r - 1].wait_recv()
+        total_b = total_b + b_in[r - 1]
+
+    for total, span in ((total_a, slice(0, CA)), (total_b, slice(CA, R))):
+        mean_grad = total * (1.0 / (NZ * NX))
+        moment = momentum_rate * moment_in[:, span] + mean_grad
+        moment_out[:, span] = moment
+        ortho[:, span] = mean_grad + momentum_rate * moment
+    stores = [pltpu.make_async_copy(moment_out, new_momentum, s_local.at[5])]
+    stores[0].start()
 
     low = 0
     for i in range(4):
@@ -322,25 +403,25 @@
             gram[j * BLOCK : (j + 1) * BLOCK, i * BLOCK : (i + 1) * BLOCK] = block.T
     ortho[...] = ortho[...] * inverse
 
-    def fill_factor():
-        now = gram[...]
-        square = exact(now, now)
+    def step(count, k, carry):
+        now = halves(gram[...], count)
+        square = mirrored(now, now)
         row_ids = lax.broadcasted_iota(jnp.int32, (R, R), 0)
         col_ids = lax.broadcasted_iota(jnp.int32, (R, R), 1)
-        factor_mat[...] = (
-            jnp.where(row_ids == col_ids, coef_one, 0.0) + coef_two * now + coef_three * square
+        factor = halves(
+            jnp.where(row_ids == col_ids, coef_one, 0.0) + coef_two * gram[...] + coef_three * square,
+            count,
         )
-
-    def step(k, carry):
-        fill_factor()
-        gram[...] = exact(gram[...], factor_mat[...])
-        gram[...] = exact(gram[...], factor_mat[...])
-        ortho[...] = exact(ortho[...], factor_mat[...])
+        ortho[...] = split_product(halves(ortho[...], count), factor)
+        if k is not None:
+            once = halves(mirrored(now, factor), count)
+            gram[...] = mirrored(once, factor)
         return carry
 
-    lax.fori_loop(0, ITERS - 1, step, 0)
-    fill_factor()
-    last = exact(ortho[...], factor_mat[...])
+    lax.fori_loop(0, FINE, functools.partial(step, 3), 0)
+    lax.fori_loop(FINE, ITERS - 1, functools.partial(step, 2), 0)
+    step(2, None, 0)
+    last = ortho[...]
 
     for copy in ml_sends:
         copy.wait_recv()
@@ -357,109 +438,113 @@
     gamma = jnp.minimum(1.0, limit / peak.astype(jnp.float32))
     scale = jnp.where(jnp.full((1, 1), d % 2, jnp.int32) == 0, jnp.sqrt(gamma), 1.0)
     update = last * (0.2 * float(max(F, R)) ** 0.5)
-    stepped = weight[...] * (1.0 - learn_rate * decay_rate) - learn_rate * update
+    stepped = weight_in[...] * (1.0 - learn_rate * decay_rate) - learn_rate * update
     master = stepped * scale
-    new_master[...] = master
+    master_out[...] = master
+    stores.append(pltpu.make_async_copy(master_out, new_master, s_local.at[6]))
     rounded[...] = master.astype(jnp.bfloat16)
 
-    local_copy = pltpu.make_async_copy(rounded, new_weight.at[z, x], s_local.at[1])
-    local_copy.start()
-    bx = [
-        send(rounded.at[CUT:BLOCK], new_weight.at[z, x, CUT:BLOCK], s_bx.at[0], r_bx.at[0], at_x(xr)),
-        send(rounded.at[CUT:BLOCK], new_weight.at[z, x, CUT:BLOCK], s_bx.at[1], r_bx.at[1], at_x(xl)),
-    ]
-    az = {}
-    az[0, 0] = send(rounded.at[0:CUT], new_weight.at[z, x, 0:CUT], s_az.at[0, 0], r_az.at[0, 0], at_z(zup))
-    az[1, 0] = send(rounded.at[0:CUT], new_weight.at[z, x, 0:CUT], s_az.at[1, 0], r_az.at[1, 0], at_z(zdn))
-
-    ax = {}
+    stores.append(pltpu.make_async_copy(rounded, new_weight.at[z, x], s_local.at[7]))
+    bx, az, ax, bz = [], {}, {}, {}
+    for r in (1, 3, 2):
+        bx.append(
+            send(
+                rounded.at[CUT:BLOCK],
+                new_weight.at[z, x, CUT:BLOCK],
+                s_bx.at[r - 1],
+                r_bx.at[r - 1],
+                at_x((x + r) % NX),
+            )
+        )
+
+    def ring_a(step):
+        up, down = (z + NZ - step) % NZ, (z + step) % NZ
+        if step == 0:
+            sources = [rounded.at[0:CUT], rounded.at[0:CUT]]
+            spans = [(0, CUT), (0, CUT)]
+        else:
+            spans = [(0, CUT), (0, CUT)] if step < 3 else [(0, 48), (48, CUT)]
+            sources = [
+                new_weight.at[up, x, spans[0][0] : spans[0][1]],
+                new_weight.at[down, x, spans[1][0] : spans[1][1]],
+            ]
+        for way, zz, to in ((0, up, zup), (1, down, zdn)):
+            lo, hi = spans[way]
+            az[way, step] = send(
+                sources[way], new_weight.at[zz, x, lo:hi], s_az.at[way, step], r_az.at[way, step], at_z(to)
+            )
+
+    def ring_b(step):
+        up, down = (z + NZ - step) % NZ, (z + step) % NZ
+        for half in range(2):
+            for way, zz, to in ((0, up, zup), (1, down, zdn)):
+                if step > 0:
+                    bz[way, step - 1, half].wait_recv()
+                if step == 3 and half != way:
+                    continue
+                piece = new_weight.at[zz, 2 * half : 2 * half + 2, CUT:BLOCK]
+                bz[way, step, half] = send(
+                    piece, piece, s_bz.at[way, step, half], r_bz.at[way, step, half], at_z(to)
+                )
 
     def spread(slot, zz, src):
         ax[slot] = [
             send(src, new_weight.at[zz, x, 0:CUT], s_ax.at[slot, 0], r_ax.at[slot, 0], at_x(xr)),
             send(src, new_weight.at[zz, x, 0:CUT], s_ax.at[slot, 1], r_ax.at[slot, 1], at_x(xl)),
         ]
-        sent.extend(ax[slot])
 
     def spread_on(slot, zz):
         ax[slot][0].wait_recv()
         left = new_weight.at[zz, xl, 0:48]
-        one = send(left, left, s_ax.at[slot, 2], r_ax.at[slot, 2], at_x(xr))
+        ax[slot].append(send(left, left, s_ax.at[slot, 2], r_ax.at[slot, 2], at_x(xr)))
         ax[slot][1].wait_recv()
         right = new_weight.at[zz, xr, 48:CUT]
-        two = send(right, right, s_ax.at[slot, 3], r_ax.at[slot, 3], at_x(xl))
-        ax[slot].extend([one, two])
-        sent.extend([one, two])
-
+        ax[slot].append(send(right, right, s_ax.at[slot, 3], r_ax.at[slot, 3], at_x(xl)))
+
+    ring_a(0)
     spread(0, z, rounded.at[0:CUT])
-    bx[0].wait_recv()
-    left = new_weight.at[z, xl, CUT : CUT + 32]
-    bx.append(send(left, left, s_bx.at[2], r_bx.at[2], at_x(xr)))
-    bx[1].wait_recv()
-    right = new_weight.at[z, xr, CUT + 32 : BLOCK]
-    bx.append(send(right, right, s_bx.at[3], r_bx.at[3], at_x(xl)))
-    local_copy.wait()
-    bx[2].wait_recv()
-    bx[3].wait_recv()
-    sent.extend(bx)
-    bz = {}
-
-    def ring_b(step):
-        if step < 3:
-            up = new_weight.at[(z + NZ - step) % NZ, :, CUT:BLOCK]
-            down = new_weight.at[(z + step) % NZ, :, CUT:BLOCK]
-        else:
-            up = new_weight.at[(z + NZ - step) % NZ, 0:2, CUT:BLOCK]
-            down = new_weight.at[(z + step) % NZ, 2:4, CUT:BLOCK]
-        bz[0, step] = send(up, up, s_bz.at[0, step], r_bz.at[0, step], at_z(zup))
-        bz[1, step] = send(down, down, s_bz.at[1, step], r_bz.at[1, step], at_z(zdn))
-        sent.extend([bz[0, step], bz[1, step]])
-
-    def ring_a(step):
-        if step < 3:
-            up = new_weight.at[(z + NZ - step) % NZ, x, 0:CUT]
-            down = new_weight.at[(z + step) % NZ, x, 0:CUT]
-        else:
-            up = new_weight.at[(z + NZ - step) % NZ, x, 0:48]
-            down = new_weight.at[(z + step) % NZ, x, 48:CUT]
-        az[0, step] = send(up, up, s_az.at[0, step], r_az.at[0, step], at_z(zup))
-        az[1, step] = send(down, down, s_az.at[1, step], r_az.at[1, step], at_z(zdn))
-
-    ring_b(0)
-    for step in range(1, 4):
+    stores[1].start()
+    stores[2].start()
+    for copy in sent:
+        copy.wait_send()
+    places = [z]
+    for step in range(1, 5):
         az[0, step - 1].wait_recv()
         az[1, step - 1].wait_recv()
-        ring_a(step)
         up, down = (z + NZ - step) % NZ, (z + step) % NZ
-        spread(2 * step - 1, up, new_weight.at[up, x, 0:CUT])
-        spread(2 * step, down, new_weight.at[down, x, 0:CUT])
+        if step < 4:
+            ring_a(step)
+            spread(2 * step - 1, up, new_weight.at[up, x, 0:CUT])
+            spread(2 * step, down, new_weight.at[down, x, 0:CUT])
+            places.extend([up, down])
+        else:
+            spread(7, up, new_weight.at[up, x, 0:CUT])
+            places.append(up)
         if step == 1:
+            stores[2].wait()
+            for copy in bx:
+                copy.wait_recv()
+        elif step == 2:
             spread_on(0, z)
         else:
-            spread_on(2 * step - 3, (z + NZ - step + 1) % NZ)
-            spread_on(2 * step - 2, (z + step - 1) % NZ)
-        bz[0, step - 1].wait_recv()
-        bz[1, step - 1].wait_recv()
-        ring_b(step)
-    az[0, 3].wait_recv()
-    az[1, 3].wait_recv()
-    far = (z + 4) % NZ
-    spread(7, far, new_weight.at[far, x, 0:CUT])
-    spread_on(5, (z + NZ - 3) % NZ)
-    spread_on(6, (z + 3) % NZ)
-    spread_on(7, far)
-    bz[0, 3].wait_recv()
-    bz[1, 3].wait_recv()
+            spread_on(2 * step - 5, places[2 * step - 5])
+            spread_on(2 * step - 4, places[2 * step - 4])
+        ring_b(step - 1)
+    for slot in range(5, 8):
+        spread_on(slot, places[slot])
+    bz[0, 3, 0].wait_recv()
+    bz[1, 3, 1].wait_recv()
     for slot in range(8):
         ax[slot][2].wait_recv()
         ax[slot][3].wait_recv()
-    sent.extend(az.values())
-    for copy in sent:
-        copy.wait_send()
+    for copies in (bx, az.values(), bz.values(), *ax.values()):
+        for copy in copies:
+            copy.wait_send()
+    stores[0].wait()
+    stores[1].wait()
 
 
 def local(grads, momentum, weight, max_logits, threshold):
-    vmem = pl.BlockSpec(memory_space=pltpu.VMEM)
     smem = pl.BlockSpec(memory_space=pltpu.SMEM)
     hbm = pl.BlockSpec(memory_space=pl.ANY)
     f32, bf16, i32 = jnp.float32, jnp.bfloat16, jnp.int32
@@ -472,14 +557,23 @@
             jax.ShapeDtypeStruct((NZ, NX, BLOCK, R), bf16),
             jax.ShapeDtypeStruct((1,), f32),
         ),
-        in_specs=[hbm, vmem, vmem, vmem, smem],
-        out_specs=(vmem, vmem, hbm, smem),
+        in_specs=[hbm, hbm, hbm, hbm, smem],
+        out_specs=(hbm, hbm, hbm, smem),
         scratch_shapes=[
-            pltpu.VMEM((NZ, BLOCK, R), bf16),
-            pltpu.VMEM((8, 3, BLOCK, R), bf16),
-            pltpu.VMEM((8, 2, BLOCK // 2, R), bf16),
-            pltpu.VMEM((2, 4, BLOCK, R), f32),
-            pltpu.VMEM((2, 4, BLOCK, R), f32),
+            pltpu.VMEM((NZ, BLOCK, CA), bf16),
+            pltpu.VMEM((NZ, NX, BLOCK, CB), bf16),
+            pltpu.VMEM((8, 3, BLOCK, CA), bf16),
+            pltpu.VMEM((2, 4, BLOCK, CA), f32),
+            pltpu.VMEM((2, 4, BLOCK, CA), f32),
+            pltpu.VMEM((2, 4, NX, BLOCK, CB), f32),
+            pltpu.VMEM((2, 4, NX, BLOCK, CB), f32),
+            pltpu.VMEM((NX, BLOCK, CB), f32),
+            pltpu.VMEM((3, BLOCK, CB), f32),
+            pltpu.VMEM((BLOCK, R), f32),
+            pltpu.VMEM((BLOCK, R), f32),
+            pltpu.VMEM((BLOCK, R), f32),
+            pltpu.VMEM((BLOCK, R), f32),
+            pltpu.VMEM((1, LAYERS, HEADS), i32),
             pltpu.VMEM((2 * HALF, BLOCK), f32),
             pltpu.VMEM((HALF, BLOCK), f32),
             pltpu.VMEM((HALF, BLOCK), f32),
@@ -490,18 +584,19 @@
             pltpu.VMEM((8, SLAB, BLOCK), f32),
             pltpu.VMEM((2 * HALF, BLOCK), f32),
             pltpu.VMEM((R, R), f32),
-            pltpu.VMEM((R, R), f32),
             pltpu.VMEM((BLOCK, R), f32),
             pltpu.VMEM((BLOCK, R), bf16),
             pltpu.VMEM((8, 128), i32),
             pltpu.VMEM((3, 8, 128), i32),
             pltpu.VMEM((8, 128), i32),
             pltpu.VMEM((7, 8, 128), i32),
-            dma((2,)),
-            dma((8, 6)),
-            dma((8, 6)),
+            dma((8,)),
+            dma((8, 3)),
+            dma((8, 3)),
             dma((2, 4)),
             dma((2, 4)),
+            dma((3, 4)),
+            dma((3, 4)),
             dma((10,)),
             dma((10,)),
             dma((30,)),
@@ -510,10 +605,10 @@
             dma((2, 4)),
             dma((8, 4)),
             dma((8, 4)),
-            dma((4,)),
-            dma((4,)),
-            dma((2, 4)),
-            dma((2, 4)),
+            dma((3,)),
+            dma((3,)),
+            dma((2, 4, 2)),
+            dma((2, 4, 2)),
         ],
         compiler_params=pltpu.CompilerParams(
             collective_id=0, has_side_effects=True, vmem_limit_bytes=48 * 1024 * 1024

time: 158 us -> 135 us (0.85)
  Pallas kernels: 148 us -> 126 us
    pallas_call x1, Pallas kernels: 148 us -> 126 us  [local(): pl.pallas_call(kernel, out_shape=(jax.ShapeDtypeStruct((BLOCK, R), f32),...]
where the time goes in v3:
time: 135 us
  Pallas kernels  126 us (93%)
  local copies, waits for them, and re-layouts  5.99 us (4%)
  between operations  3.04 us (2%)
    pallas_call x1, Pallas kernels, local(): pl.pallas_call(kernel, out_shape=(jax.ShapeDtypeStruct((BLOCK, R), f32),...  126 us
    unnamed x9, local copies, waits for them, and re-layouts  5.99 us

profile of v3, /device:TPU:1, one launch (start us, length us, event | category | flops | bytes accessed | tf_op | source)
XLA Modules:
  0.0 135.0 jit_solution(13925892881063724215)
XLA Ops:
  1.3 0.0 copy-start
  1.3 0.9 copy-done
  2.2 0.0 copy-start.1
  2.2 0.9 copy-done.1
  3.2 0.0 copy-start.2
  3.2 0.7 copy-done.2
  3.9 125.9 %muon.1 = (f32[128,512]{1,0:T(8,128)S(1)}, f32[128,512]{1,0:T(8,128)S(1)}, bf16[8,4,128,512]{3,2,1,0:T(8,128)(2,1)S(1)}, f32[1]{0:T(128)}) custom-call(bf16[8,4,128,512]{3,2,1,0:T(8,128)(2,1)} %bitcast.3, f32[128,512]{1,0:T(8,128)S(1)} %copy-done, f32[128,512]{1,0:T(8,128)S(1)} %copy-done.1, s32[1,2,64]{2,1,0:T(2,128)S(1)} %copy-done.2, s32[1]{0:T(128)S(6)} %copy.13.threshold), custom_call_target="tpu_custom_call" | custom-call | tf_op jit(solution)/shard_map/muon/pallas_call | solution.py:552
  129.8 0.7 copy.14
  130.5 0.7 copy.15
  131.2 2.0 %copy.16 = bf16[4096,512]{1,0:T(8,128)(2,1)} copy(bf16[4096,512]{1,0:T(8,128)(2,1)S(1)} %bitcast.2) | data formatting | bytes 8388608
Async XLA Ops:
  1.3 1.0 copy-start
  2.2 0.9 copy-start.1
  3.2 0.7 copy-start.2

commit v4 on v3

--- a/solution.py
+++ b/solution.py
@@ -92,6 +92,7 @@
     zr,
     bs,
     br,
+    b_raw,
     b_sum,
     b_in,
     moment_in,
@@ -169,6 +170,11 @@
 
     sent = []
 
+    def drain(copies):
+        for copy in copies:
+            copy.wait_send()
+        del sent[: len(copies)]
+
     barrier = pltpu.get_barrier_semaphore()
     mates = [at_xy((m8 + r) % 8) for r in range(1, 8)]
     mates += [at_z((z + r) % NZ) for r in range(1, NZ)]
@@ -251,13 +257,14 @@
             zt = (z + sign * (4 - step) + NZ) % NZ
             lo, up = 2 * way, 2 * way + 2
             if step == 0:
-                bs[way, 0, lo:up] = own_b[zt, lo:up].astype(jnp.float32)
-                src, dst = bs.at[way, 0, lo:up], br.at[way, 0, lo:up]
+                src, dst = grads.at[zt, lo:up, :, CA:R], b_raw.at[way]
             else:
                 wheel[way, step - 1].wait_recv()
                 if step == 1:
                     rest = 2 - lo
-                    bs[way, 1, lo:up] = own_b[zt, lo:up].astype(jnp.float32) + br[way, 0, lo:up]
+                    bs[way, 1, lo:up] = own_b[zt, lo:up].astype(jnp.float32) + b_raw[way].astype(
+                        jnp.float32
+                    )
                     bs[way, 1, rest : rest + 2] = own_b[zt, rest : rest + 2].astype(jnp.float32)
                 else:
                     bs[way, step] = own_b[zt].astype(jnp.float32) + br[way, step - 1]
@@ -265,10 +272,9 @@
             wheel[way, step] = send(src, dst, s_b.at[way, step], r_b.at[way, step], at_z(to))
             sent.append(wheel[way, step])
 
+    turn(0)
     start_chunk(0)
     start_chunk(1)
-    loads[0].wait()
-    turn(0)
     start_chunk(2)
     loads[2].wait()
     ml_out[...] = jnp.zeros_like(ml_out)
@@ -279,14 +285,16 @@
             send(ml_out, ml_x.at[r - 1], s_ml.at[r - 1], r_ml.at[r - 1], at_x((x + r) % NX))
         )
     sent.extend(ml_sends)
+    loads[0].wait()
+    turn(1)
     loads[1].wait()
     cross = []
     for j in range(7):
         finish_chunk(j)
         if j + 3 < 8:
             start_chunk(j + 3)
-        if j in (0, 2, 4):
-            turn(j // 2 + 1)
+        if j in (0, 3):
+            turn(2 if j == 0 else 3)
         if j == 3:
             for copy in ml_sends:
                 copy.wait_recv()
@@ -331,21 +339,26 @@
         for j in range(i, 4):
             packed[low * BLOCK : (low + 1) * BLOCK] = strip[:, (j - i) * BLOCK : (j - i + 1) * BLOCK]
             low += 1
-    theirs = pl.ds(pl.multiple_of((1 - core) * HALF, BLOCK // 2), HALF)
-    mine = pl.ds(pl.multiple_of(core * HALF, BLOCK // 2), HALF)
-    copy = send(packed.at[theirs], core_in, s_g.at[0], r_g.at[0], partner)
-    sent.append(copy)
-    copy.wait_recv()
-    half_sum[...] = packed[mine] + core_in[...]
-
+    def piece_of(which, p):
+        return pl.ds(pl.multiple_of(which * HALF + p * PART, 8), PART)
+
+    mates = [(m8 + r) % 8 for r in range(8)]
+    swaps = []
+    for r in (1, 2, 3, 4, 5, 6, 7, 0):
+        p = mates[r]
+        swaps.append(
+            send(packed.at[piece_of(1 - core, p)], core_in.at[r], s_g.at[r], r_g.at[r], partner)
+        )
+    sent.extend(swaps)
     copies = []
     for r in range(1, 8):
-        p = (m8 + r) % 8
-        piece = pl.ds(pl.multiple_of(p * PART, 8), PART)
-        copies.append(send(half_sum.at[piece], xy_in.at[r - 1], s_g.at[r], r_g.at[r], at_xy(p)))
+        p = mates[r]
+        swaps[r - 1].wait_recv()
+        half_sum[r] = packed[piece_of(core, p)] + core_in[r]
+        copies.append(send(half_sum.at[r], xy_in.at[r - 1], s_g.at[7 + r], r_g.at[7 + r], at_xy(p)))
     sent.extend(copies)
-    my_piece = pl.ds(pl.multiple_of(m8 * PART, 8), PART)
-    part = half_sum[my_piece]
+    swaps[7].wait_recv()
+    part = packed[piece_of(core, m8)] + core_in[0]
     for r in range(1, 8):
         copies[r - 1].wait_recv()
         part = part + xy_in[r - 1]
@@ -355,9 +368,10 @@
     for r in range(1, NZ):
         zt = (z + r) % NZ
         copies.append(
-            send(slab_out.at[zt], slab_in.at[r - 1], s_g.at[7 + r], r_g.at[7 + r], at_z(zt))
+            send(slab_out.at[zt], slab_in.at[r - 1], s_g.at[14 + r], r_g.at[14 + r], at_z(zt))
         )
     sent.extend(copies)
+    drain(sent[:-7])
     slab = slab_out[z]
     for r in range(1, NZ):
         copies[r - 1].wait_recv()
@@ -368,23 +382,27 @@
     for r in range(1, NZ):
         zt = (z + r) % NZ
         copies.append(
-            send(slab_sum, slab_all.at[z], s_g.at[14 + r], r_g.at[14 + r], at_z(zt))
+            send(slab_sum, slab_all.at[z], s_g.at[21 + r], r_g.at[21 + r], at_z(zt))
         )
     sent.extend(copies)
     for copy in copies:
         copy.wait_recv()
-    here = pl.ds(pl.multiple_of(core * HALF + m8 * PART, 8), PART)
+    here = piece_of(core, m8)
     full[here] = jnp.concatenate([slab_all[i] for i in range(8)], axis=0)
     copies = []
     for r in range(1, 8):
-        p = (m8 + r) % 8
-        copies.append(send(full.at[here], full.at[here], s_g.at[21 + r], r_g.at[21 + r], at_xy(p)))
+        copies.append(
+            send(full.at[here], full.at[here], s_g.at[28 + r], r_g.at[28 + r], at_xy(mates[r]))
+        )
+    swaps = [send(full.at[here], full.at[here], s_g.at[36], r_g.at[36], partner)]
+    for r in range(1, 8):
+        copies[r - 1].wait_recv()
+        there = piece_of(core, (m8 + 8 - r) % 8)
+        swaps.append(send(full.at[there], full.at[there], s_g.at[36 + r], r_g.at[36 + r], partner))
+    for copy in swaps:
+        copy.wait_recv()
     sent.extend(copies)
-    for copy in copies:
-        copy.wait_recv()
-    copy = send(full.at[mine], full.at[mine], s_g.at[29], r_g.at[29], partner)
-    sent.append(copy)
-    copy.wait_recv()
+    sent.extend(swaps)
 
     rows = lax.broadcasted_iota(jnp.int32, (BLOCK, BLOCK), 0)
     cols = lax.broadcasted_iota(jnp.int32, (BLOCK, BLOCK), 1)
@@ -405,14 +423,14 @@
 
     def step(count, k, carry):
         now = halves(gram[...], count)
-        square = mirrored(now, now)
+        square = mirrored(now[:2], now[:2])
         row_ids = lax.broadcasted_iota(jnp.int32, (R, R), 0)
         col_ids = lax.broadcasted_iota(jnp.int32, (R, R), 1)
         factor = halves(
             jnp.where(row_ids == col_ids, coef_one, 0.0) + coef_two * gram[...] + coef_three * square,
             count,
         )
-        ortho[...] = split_product(halves(ortho[...], count), factor)
+        ortho[...] = split_product(halves(ortho[...], 2), factor[:2])
         if k is not None:
             once = halves(mirrored(now, factor), count)
             gram[...] = mirrored(once, factor)
@@ -505,8 +523,7 @@
     spread(0, z, rounded.at[0:CUT])
     stores[1].start()
     stores[2].start()
-    for copy in sent:
-        copy.wait_send()
+    drain(sent[:])
     places = [z]
     for step in range(1, 5):
         az[0, step - 1].wait_recv()
@@ -567,6 +584,7 @@
             pltpu.VMEM((2, 4, BLOCK, CA), f32),
             pltpu.VMEM((2, 4, NX, BLOCK, CB), f32),
             pltpu.VMEM((2, 4, NX, BLOCK, CB), f32),
+            pltpu.VMEM((2, 2, BLOCK, CB), bf16),
             pltpu.VMEM((NX, BLOCK, CB), f32),
             pltpu.VMEM((3, BLOCK, CB), f32),
             pltpu.VMEM((BLOCK, R), f32),
@@ -575,8 +593,8 @@
             pltpu.VMEM((BLOCK, R), f32),
             pltpu.VMEM((1, LAYERS, HEADS), i32),
             pltpu.VMEM((2 * HALF, BLOCK), f32),
-            pltpu.VMEM((HALF, BLOCK), f32),
-            pltpu.VMEM((HALF, BLOCK), f32),
+            pltpu.VMEM((8, PART, BLOCK), f32),
+            pltpu.VMEM((8, PART, BLOCK), f32),
             pltpu.VMEM((7, PART, BLOCK), f32),
             pltpu.VMEM((8, SLAB, BLOCK), f32),
             pltpu.VMEM((7, SLAB, BLOCK), f32),
@@ -599,8 +617,8 @@
             dma((3, 4)),
             dma((10,)),
             dma((10,)),
-            dma((30,)),
-            dma((30,)),
+            dma((44,)),
+            dma((44,)),
             dma((2, 4)),
             dma((2, 4)),
             dma((8, 4)),

time: 135 us -> 130 us (0.963)
  Pallas kernels: 126 us -> 121 us
    pallas_call x1, Pallas kernels: 126 us -> 121 us  [local(): pl.pallas_call(kernel, out_shape=(jax.ShapeDtypeStruct((BLOCK, R), f32),...]
where the time goes in v4:
time: 130 us
  Pallas kernels  121 us (93%)
  local copies, waits for them, and re-layouts  5.99 us (5%)
  between operations  3.04 us (2%)
    pallas_call x1, Pallas kernels, local(): pl.pallas_call(kernel, out_shape=(jax.ShapeDtypeStruct((BLOCK, R), f32),...  121 us
    unnamed x9, local copies, waits for them, and re-layouts  5.99 us

profile of v4, /device:TPU:1, one launch (start us, length us, event | category | flops | bytes accessed | tf_op | source)
XLA Modules:
  0.0 129.7 jit_solution(16398240670688056971)
XLA Ops:
  1.3 0.0 copy-start
  1.3 0.9 copy-done
  2.2 0.0 copy-start.1
  2.2 0.9 copy-done.1
  3.2 0.0 copy-start.2
  3.2 0.7 copy-done.2
  3.9 120.6 %muon.1 = (f32[128,512]{1,0:T(8,128)S(1)}, f32[128,512]{1,0:T(8,128)S(1)}, bf16[8,4,128,512]{3,2,1,0:T(8,128)(2,1)S(1)}, f32[1]{0:T(128)}) custom-call(bf16[8,4,128,512]{3,2,1,0:T(8,128)(2,1)} %bitcast.3, f32[128,512]{1,0:T(8,128)S(1)} %copy-done, f32[128,512]{1,0:T(8,128)S(1)} %copy-done.1, s32[1,2,64]{2,1,0:T(2,128)S(1)} %copy-done.2, s32[1]{0:T(128)S(6)} %copy.13.threshold), custom_call_target="tpu_custom_call" | custom-call | tf_op jit(solution)/shard_map/muon/pallas_call | solution.py:569
  124.5 0.7 copy.14
  125.2 0.7 copy.15
  125.9 2.0 %copy.16 = bf16[4096,512]{1,0:T(8,128)(2,1)} copy(bf16[4096,512]{1,0:T(8,128)(2,1)S(1)} %bitcast.2) | data formatting | bytes 8388608
Async XLA Ops:
  1.3 1.0 copy-start
  2.2 0.9 copy-start.1
  3.2 0.7 copy-start.2

commit v5 on v4

--- a/solution.py
+++ b/solution.py
@@ -35,8 +35,7 @@
 ORDER = (4, -3, 3, -2, 2, -1, 1, 0)
 PAIRS = [(i, j) for i in range(4) for j in range(i, 4)]
 HALF = len(PAIRS) * BLOCK // 2
-PART = HALF // 8
-SLAB = PART // 8
+PART = HALF // 16
 
 
 def exact(left, right, dims=((1,), (0,))):
@@ -103,11 +102,9 @@
     packed,
     core_in,
     half_sum,
-    xy_in,
-    slab_out,
-    slab_in,
-    slab_sum,
-    slab_all,
+    group_in,
+    mid,
+    row_in,
     full,
     gram,
     ortho,
@@ -115,6 +112,7 @@
     ml_out,
     ml_x,
     ml_mid,
+    ml_pair,
     ml_z,
     s_local,
     s_x,
@@ -143,7 +141,8 @@
     ybase = (y // 2) * 2
     xr, xl, xo = (x + 1) % NX, (x + 3) % NX, (x + 2) % NX
     zup, zdn = (z + 1) % NZ, (z + NZ - 1) % NZ
-    m8 = x * 2 + y % 2
+    m16 = (x * 2 + y % 2) * 2 + z % 2
+    zpair = (z // 2) * 2
 
     def at_x(xx):
         return (z * NX + xx, c)
@@ -151,8 +150,8 @@
     def at_z(zz):
         return (zz * NX + x, c)
 
-    def at_xy(p):
-        return (z * NX + p // 2, (ybase + p % 2) * 2 + core)
+    def at_group(p):
+        return ((zpair + p % 2) * NX + p // 4, (ybase + (p // 2) % 2) * 2 + core)
 
     partner = (d, y * 2 + 1 - core)
 
@@ -176,9 +175,9 @@
         del sent[: len(copies)]
 
     barrier = pltpu.get_barrier_semaphore()
-    mates = [at_xy((m8 + r) % 8) for r in range(1, 8)]
-    mates += [at_z((z + r) % NZ) for r in range(1, NZ)]
-    mates += [partner]
+    mates = [at_group((m16 + r) % 16) for r in range(1, 16)]
+    mates += [at_z((z + r) % NZ) for r in (2, 4, 6)]
+    mates += [at_z((z + 7 - 6 * (z % 2)) % NZ), partner]
     for mate in mates:
         pl.semaphore_signal(
             barrier, inc=1, device_id=mate, device_id_type=pl.DeviceIdType.MESH
@@ -301,11 +300,7 @@
             ml_mid[...] = jnp.maximum(
                 jnp.maximum(ml_out[...], ml_x[0]), jnp.maximum(ml_x[1], ml_x[2])
             )
-            ml_sends = []
-            for r in range(1, NZ):
-                ml_sends.append(
-                    send(ml_mid, ml_z.at[r - 1], s_ml.at[r + 2], r_ml.at[r + 2], at_z((z + r) % NZ))
-                )
+            ml_sends = [send(ml_mid, ml_z.at[0], s_ml.at[3], r_ml.at[3], at_z(zpair + 1 - z % 2))]
             sent.extend(ml_sends)
         if j == 5:
             wheel[0, 3].wait_recv()
@@ -317,6 +312,14 @@
                     send(b_sum.at[xt], b_in.at[r - 1], s_b.at[2, r - 1], r_b.at[2, r - 1], at_x(xt))
                 )
             sent.extend(cross)
+            ml_sends[0].wait_recv()
+            ml_pair[...] = jnp.maximum(ml_mid[...], ml_z[0])
+            ml_sends = []
+            for k in range(1, 4):
+                ml_sends.append(
+                    send(ml_pair, ml_z.at[k], s_ml.at[3 + k], r_ml.at[3 + k], at_z((z + 2 * k) % NZ))
+                )
+            sent.extend(ml_sends)
     total_a = finish_chunk(7)
     loads[3].wait()
     loads[4].wait()
@@ -339,66 +342,51 @@
         for j in range(i, 4):
             packed[low * BLOCK : (low + 1) * BLOCK] = strip[:, (j - i) * BLOCK : (j - i + 1) * BLOCK]
             low += 1
+
     def piece_of(which, p):
         return pl.ds(pl.multiple_of(which * HALF + p * PART, 8), PART)
 
-    mates = [(m8 + r) % 8 for r in range(8)]
-    swaps = []
-    for r in (1, 2, 3, 4, 5, 6, 7, 0):
-        p = mates[r]
-        swaps.append(
-            send(packed.at[piece_of(1 - core, p)], core_in.at[r], s_g.at[r], r_g.at[r], partner)
-        )
-    sent.extend(swaps)
+    mine = pl.ds(pl.multiple_of(core * HALF, 8), HALF)
+    theirs = pl.ds(pl.multiple_of((1 - core) * HALF, 8), HALF)
+    swap = send(packed.at[theirs], core_in, s_g.at[0], r_g.at[0], partner)
+    swap.wait_recv()
+    half_sum[...] = packed[mine] + core_in[...]
     copies = []
-    for r in range(1, 8):
-        p = mates[r]
-        swaps[r - 1].wait_recv()
-        half_sum[r] = packed[piece_of(core, p)] + core_in[r]
-        copies.append(send(half_sum.at[r], xy_in.at[r - 1], s_g.at[7 + r], r_g.at[7 + r], at_xy(p)))
-    sent.extend(copies)
-    swaps[7].wait_recv()
-    part = packed[piece_of(core, m8)] + core_in[0]
-    for r in range(1, 8):
+    for r in range(1, 16):
+        p = (m16 + r) % 16
+        copies.append(
+            send(half_sum.at[piece_of(0, p)], group_in.at[r - 1], s_g.at[r], r_g.at[r], at_group(p))
+        )
+    drain(sent[:])
+    sent.extend([swap] + copies)
+    part = half_sum[piece_of(0, m16)]
+    for r in range(1, 16):
         copies[r - 1].wait_recv()
-        part = part + xy_in[r - 1]
-    for i in range(8):
-        slab_out[i] = part[i * SLAB : (i + 1) * SLAB]
+        part = part + group_in[r - 1]
+    mid[...] = part
+    row_in[z // 2] = part
     copies = []
-    for r in range(1, NZ):
-        zt = (z + r) % NZ
+    for k in range(1, 4):
         copies.append(
-            send(slab_out.at[zt], slab_in.at[r - 1], s_g.at[14 + r], r_g.at[14 + r], at_z(zt))
-        )
-    sent.extend(copies)
-    drain(sent[:-7])
-    slab = slab_out[z]
-    for r in range(1, NZ):
-        copies[r - 1].wait_recv()
-        slab = slab + slab_in[r - 1]
-    slab_sum[...] = slab
-    slab_all[z] = slab
-    copies = []
-    for r in range(1, NZ):
-        zt = (z + r) % NZ
-        copies.append(
-            send(slab_sum, slab_all.at[z], s_g.at[21 + r], r_g.at[21 + r], at_z(zt))
-        )
-    sent.extend(copies)
+            send(mid, row_in.at[z // 2], s_g.at[15 + k], r_g.at[15 + k], at_z((z + 2 * k) % NZ))
+        )
     for copy in copies:
         copy.wait_recv()
-    here = piece_of(core, m8)
-    full[here] = jnp.concatenate([slab_all[i] for i in range(8)], axis=0)
+    sent.extend(copies)
+    here = piece_of(core, m16)
+    full[here] = (row_in[0] + row_in[1]) + (row_in[2] + row_in[3])
     copies = []
-    for r in range(1, 8):
+    for r in range(1, 16):
         copies.append(
-            send(full.at[here], full.at[here], s_g.at[28 + r], r_g.at[28 + r], at_xy(mates[r]))
-        )
-    swaps = [send(full.at[here], full.at[here], s_g.at[36], r_g.at[36], partner)]
-    for r in range(1, 8):
+            send(
+                full.at[here], full.at[here], s_g.at[18 + r], r_g.at[18 + r], at_group((m16 + r) % 16)
+            )
+        )
+    swaps = [send(full.at[here], full.at[here], s_g.at[34], r_g.at[34], partner)]
+    for r in range(1, 16):
         copies[r - 1].wait_recv()
-        there = piece_of(core, (m8 + 8 - r) % 8)
-        swaps.append(send(full.at[there], full.at[there], s_g.at[36 + r], r_g.at[36 + r], partner))
+        there = piece_of(core, (m16 + 16 - r) % 16)
+        swaps.append(send(full.at[there], full.at[there], s_g.at[34 + r], r_g.at[34 + r], partner))
     for copy in swaps:
         copy.wait_recv()
     sent.extend(copies)
@@ -443,9 +431,9 @@
 
     for copy in ml_sends:
         copy.wait_recv()
-    peaks = ml_mid[...]
-    for r in range(NZ - 1):
-        peaks = jnp.maximum(peaks, ml_z[r])
+    peaks = ml_pair[...]
+    for k in range(1, 4):
+        peaks = jnp.maximum(peaks, ml_z[k])
     head = (c % (2 * NY // LAYERS)) * (HEADS * LAYERS // (2 * NY)) + d // 2
     layer = c // (2 * NY // LAYERS)
     rows = lax.broadcasted_iota(jnp.int32, (8, 128), 0)
@@ -475,35 +463,39 @@
             )
         )
 
-    def ring_a(step):
-        up, down = (z + NZ - step) % NZ, (z + step) % NZ
-        if step == 0:
-            sources = [rounded.at[0:CUT], rounded.at[0:CUT]]
-            spans = [(0, CUT), (0, CUT)]
-        else:
-            spans = [(0, CUT), (0, CUT)] if step < 3 else [(0, 48), (48, CUT)]
-            sources = [
-                new_weight.at[up, x, spans[0][0] : spans[0][1]],
-                new_weight.at[down, x, spans[1][0] : spans[1][1]],
-            ]
-        for way, zz, to in ((0, up, zup), (1, down, zdn)):
-            lo, hi = spans[way]
-            az[way, step] = send(
-                sources[way], new_weight.at[zz, x, lo:hi], s_az.at[way, step], r_az.at[way, step], at_z(to)
-            )
-
-    def ring_b(step):
-        up, down = (z + NZ - step) % NZ, (z + step) % NZ
-        for half in range(2):
-            for way, zz, to in ((0, up, zup), (1, down, zdn)):
-                if step > 0:
-                    bz[way, step - 1, half].wait_recv()
-                if step == 3 and half != way:
-                    continue
-                piece = new_weight.at[zz, 2 * half : 2 * half + 2, CUT:BLOCK]
-                bz[way, step, half] = send(
-                    piece, piece, s_bz.at[way, step, half], r_bz.at[way, step, half], at_z(to)
-                )
+    def first_a(distance):
+        for way, to in ((0, (z + distance) % NZ), (1, (z + NZ - distance) % NZ)):
+            az[way, distance] = send(
+                rounded.at[0:CUT],
+                new_weight.at[z, x, 0:CUT],
+                s_az.at[way, distance - 1],
+                r_az.at[way, distance - 1],
+                at_z(to),
+            )
+
+    def ring_a(distance):
+        for way, zz, to in (
+            (0, (z + NZ - distance + 1) % NZ, zup),
+            (1, (z + distance - 1) % NZ, zdn),
+        ):
+            lo, hi = (0, CUT) if distance < 4 else ((0, 48) if way == 0 else (48, CUT))
+            piece = new_weight.at[zz, x, lo:hi]
+            az[way, distance] = send(
+                piece, piece, s_az.at[way, distance - 1], r_az.at[way, distance - 1], at_z(to)
+            )
+
+    def ring_b(step, r):
+        xx = (x + r) % NX
+        for way, zz, to in ((0, (z + NZ - step) % NZ, zup), (1, (z + step) % NZ, zdn)):
+            if step > 0:
+                bz[way, step - 1, r].wait_recv()
+            if step == 3 and (r < 2) != (way == 0):
+                continue
+            piece = new_weight.at[zz, xx, CUT:BLOCK]
+            src = rounded.at[CUT:BLOCK] if step == 0 and r == 0 else piece
+            bz[way, step, r] = send(
+                src, piece, s_bz.at[way, step, r], r_bz.at[way, step, r], at_z(to)
+            )
 
     def spread(slot, zz, src):
         ax[slot] = [
@@ -519,38 +511,57 @@
         right = new_weight.at[zz, xr, 48:CUT]
         ax[slot].append(send(right, right, s_ax.at[slot, 3], r_ax.at[slot, 3], at_x(xl)))
 
-    ring_a(0)
+    first_a(1)
+    first_a(2)
     spread(0, z, rounded.at[0:CUT])
+    ring_b(0, 0)
     stores[1].start()
     stores[2].start()
     drain(sent[:])
     places = [z]
-    for step in range(1, 5):
-        az[0, step - 1].wait_recv()
-        az[1, step - 1].wait_recv()
-        up, down = (z + NZ - step) % NZ, (z + step) % NZ
-        if step < 4:
-            ring_a(step)
-            spread(2 * step - 1, up, new_weight.at[up, x, 0:CUT])
-            spread(2 * step, down, new_weight.at[down, x, 0:CUT])
-            places.extend([up, down])
-        else:
-            spread(7, up, new_weight.at[up, x, 0:CUT])
-            places.append(up)
-        if step == 1:
-            stores[2].wait()
-            for copy in bx:
-                copy.wait_recv()
-        elif step == 2:
-            spread_on(0, z)
-        else:
-            spread_on(2 * step - 5, places[2 * step - 5])
-            spread_on(2 * step - 4, places[2 * step - 4])
-        ring_b(step - 1)
-    for slot in range(5, 8):
-        spread_on(slot, places[slot])
-    bz[0, 3, 0].wait_recv()
-    bz[1, 3, 1].wait_recv()
+    for k in range(1, 4):
+        places.extend([(z + NZ - k) % NZ, (z + k) % NZ])
+    places.append((z + 4) % NZ)
+
+    def arrived(distance):
+        az[0, distance].wait_recv()
+        az[1, distance].wait_recv()
+
+    def spread_two(k):
+        for slot in (2 * k - 1, 2 * k):
+            spread(slot, places[slot], new_weight.at[places[slot], x, 0:CUT])
+
+    arrived(1)
+    spread_two(1)
+    arrived(2)
+    ring_a(3)
+    spread_two(2)
+    for r in (1, 3, 2):
+        bx[(3, 1, 2).index(r)].wait_recv()
+        ring_b(0, r)
+    spread_on(0, z)
+    ring_b(1, 0)
+    arrived(3)
+    ring_a(4)
+    spread_two(3)
+    spread_on(1, places[1])
+    spread_on(2, places[2])
+    for r in (1, 3, 2):
+        ring_b(1, r)
+    arrived(4)
+    spread(7, places[7], new_weight.at[places[7], x, 0:CUT])
+    spread_on(3, places[3])
+    spread_on(4, places[4])
+    for r in (0, 1, 3, 2):
+        ring_b(2, r)
+    spread_on(5, places[5])
+    spread_on(6, places[6])
+    for r in (0, 1, 3, 2):
+        ring_b(3, r)
+    spread_on(7, places[7])
+    for r in range(4):
+        bz[r // 2, 3, r].wait_recv()
+    stores[2].wait()
     for slot in range(8):
         ax[slot][2].wait_recv()
         ax[slot][3].wait_recv()
@@ -593,13 +604,11 @@
             pltpu.VMEM((BLOCK, R), f32),
             pltpu.VMEM((1, LAYERS, HEADS), i32),
             pltpu.VMEM((2 * HALF, BLOCK), f32),
-            pltpu.VMEM((8, PART, BLOCK), f32),
-            pltpu.VMEM((8, PART, BLOCK), f32),
-            pltpu.VMEM((7, PART, BLOCK), f32),
-            pltpu.VMEM((8, SLAB, BLOCK), f32),
-            pltpu.VMEM((7, SLAB, BLOCK), f32),
-            pltpu.VMEM((SLAB, BLOCK), f32),
-            pltpu.VMEM((8, SLAB, BLOCK), f32),
+            pltpu.VMEM((HALF, BLOCK), f32),
+            pltpu.VMEM((HALF, BLOCK), f32),
+            pltpu.VMEM((15, PART, BLOCK), f32),
+            pltpu.VMEM((PART, BLOCK), f32),
+            pltpu.VMEM((4, PART, BLOCK), f32),
             pltpu.VMEM((2 * HALF, BLOCK), f32),
             pltpu.VMEM((R, R), f32),
             pltpu.VMEM((BLOCK, R), f32),
@@ -607,7 +616,8 @@
             pltpu.VMEM((8, 128), i32),
             pltpu.VMEM((3, 8, 128), i32),
             pltpu.VMEM((8, 128), i32),
-            pltpu.VMEM((7, 8, 128), i32),
+            pltpu.VMEM((8, 128), i32),
+            pltpu.VMEM((4, 8, 128), i32),
             dma((8,)),
             dma((8, 3)),
             dma((8, 3)),
@@ -617,16 +627,16 @@
             dma((3, 4)),
             dma((10,)),
             dma((10,)),
-            dma((44,)),
-            dma((44,)),
+            dma((50,)),
+            dma((50,)),
             dma((2, 4)),
             dma((2, 4)),
             dma((8, 4)),
             dma((8, 4)),
             dma((3,)),
             dma((3,)),
-            dma((2, 4, 2)),
-            dma((2, 4, 2)),
+            dma((2, 4, 4)),
+            dma((2, 4, 4)),
         ],
         compiler_params=pltpu.CompilerParams(
             collective_id=0, has_side_effects=True, vmem_limit_bytes=48 * 1024 * 1024

time: 130 us -> 126 us (0.969)
  Pallas kernels: 121 us -> 116 us
    pallas_call x1, Pallas kernels: 121 us -> 116 us  [local(): pl.pallas_call(kernel, out_shape=(jax.ShapeDtypeStruct((BLOCK, R), f32),...]
where the time goes in v5:
time: 126 us; the launch traced here: 125 us
  Pallas kernels  116 us (92%)
  local copies, waits for them, and re-layouts  5.99 us (5%)
  between operations  3.04 us (2%)
    pallas_call x1, Pallas kernels, local(): pl.pallas_call(kernel, out_shape=(jax.ShapeDtypeStruct((BLOCK, R), f32),...  116 us
    unnamed x9, local copies, waits for them, and re-layouts  5.99 us

profile of v5, /device:TPU:1, one launch (start us, length us, event | category | flops | bytes accessed | tf_op | source)
XLA Modules:
  0.0 125.5 jit_solution(6128639288795062504)
XLA Ops:
  1.3 0.0 copy-start
  1.3 0.9 copy-done
  2.2 0.0 copy-start.1
  2.2 0.9 copy-done.1
  3.2 0.0 copy-start.2
  3.2 0.7 copy-done.2
  3.9 116.5 %muon.1 = (f32[128,512]{1,0:T(8,128)S(1)}, f32[128,512]{1,0:T(8,128)S(1)}, bf16[8,4,128,512]{3,2,1,0:T(8,128)(2,1)S(1)}, f32[1]{0:T(128)}) custom-call(bf16[8,4,128,512]{3,2,1,0:T(8,128)(2,1)} %bitcast.3, f32[128,512]{1,0:T(8,128)S(1)} %copy-done, f32[128,512]{1,0:T(8,128)S(1)} %copy-done.1, s32[1,2,64]{2,1,0:T(2,128)S(1)} %copy-done.2, s32[1]{0:T(128)S(6)} %copy.13.threshold), custom_call_target="tpu_custom_call" | custom-call | tf_op jit(solution)/shard_map/muon/pallas_call | solution.py:580
  120.3 0.7 copy.14
  121.0 0.7 copy.15
  121.7 2.0 %copy.16 = bf16[4096,512]{1,0:T(8,128)(2,1)} copy(bf16[4096,512]{1,0:T(8,128)(2,1)S(1)} %bitcast.2) | data formatting | bytes 8388608
Async XLA Ops:
  1.3 1.0 copy-start
  2.2 0.9 copy-start.1
  3.2 0.7 copy-start.2

commit v6 on v5

--- a/solution.py
+++ b/solution.py
@@ -114,6 +114,7 @@
     ml_mid,
     ml_pair,
     ml_z,
+    plane,
     s_local,
     s_x,
     r_x,
@@ -175,9 +176,8 @@
         del sent[: len(copies)]
 
     barrier = pltpu.get_barrier_semaphore()
-    mates = [at_group((m16 + r) % 16) for r in range(1, 16)]
-    mates += [at_z((z + r) % NZ) for r in (2, 4, 6)]
-    mates += [at_z((z + 7 - 6 * (z % 2)) % NZ), partner]
+    across = (d, (ybase + 1 - y % 2) * 2 + core)
+    mates = [at_x(xr), at_x(xl), at_x(xo), at_z(zup), at_z(zdn), across, partner]
     for mate in mates:
         pl.semaphore_signal(
             barrier, inc=1, device_id=mate, device_id_type=pl.DeviceIdType.MESH
@@ -302,6 +302,10 @@
             )
             ml_sends = [send(ml_mid, ml_z.at[0], s_ml.at[3], r_ml.at[3], at_z(zpair + 1 - z % 2))]
             sent.extend(ml_sends)
+        if j == 4:
+            pl.semaphore_signal(
+                plane, inc=1, device_id=across, device_id_type=pl.DeviceIdType.MESH
+            )
         if j == 5:
             wheel[0, 3].wait_recv()
             wheel[1, 3].wait_recv()
@@ -351,6 +355,7 @@
     swap = send(packed.at[theirs], core_in, s_g.at[0], r_g.at[0], partner)
     swap.wait_recv()
     half_sum[...] = packed[mine] + core_in[...]
+    pl.semaphore_wait(plane, 1)
     copies = []
     for r in range(1, 16):
         p = (m16 + r) % 16
@@ -419,15 +424,17 @@
             count,
         )
         ortho[...] = split_product(halves(ortho[...], 2), factor[:2])
-        if k is not None:
-            once = halves(mirrored(now, factor), count)
-            gram[...] = mirrored(once, factor)
+        once = halves(mirrored(now, factor), count)
+        gram[...] = mirrored(once, factor)
         return carry
 
     lax.fori_loop(0, FINE, functools.partial(step, 3), 0)
     lax.fori_loop(FINE, ITERS - 1, functools.partial(step, 2), 0)
-    step(2, None, 0)
-    last = ortho[...]
+    now = halves(gram[...], 2)
+    first = ortho[...]
+    second = split_product(halves(first, 2), now)
+    third = split_product(halves(second, 2), now)
+    last = coef_one * first + coef_two * second + coef_three * third
 
     for copy in ml_sends:
         copy.wait_recv()
@@ -618,6 +625,7 @@
             pltpu.VMEM((8, 128), i32),
             pltpu.VMEM((8, 128), i32),
             pltpu.VMEM((4, 8, 128), i32),
+            pltpu.SemaphoreType.REGULAR,
             dma((8,)),
             dma((8, 3)),
             dma((8, 3)),

time: 126 us -> 124 us (0.984)
  Pallas kernels: 116 us -> 114 us
    pallas_call x1, Pallas kernels: 116 us -> 114 us  [local(): pl.pallas_call(kernel, out_shape=(jax.ShapeDtypeStruct((BLOCK, R), f32),...]
where the time goes in v6:
time: 124 us
  Pallas kernels  114 us (92%)
  local copies, waits for them, and re-layouts  5.99 us (5%)
  between operations  3.04 us (2%)
    pallas_call x1, Pallas kernels, local(): pl.pallas_call(kernel, out_shape=(jax.ShapeDtypeStruct((BLOCK, R), f32),...  114 us
    unnamed x9, local copies, waits for them, and re-layouts  5.99 us

profile of v6, /device:TPU:1, one launch (start us, length us, event | category | flops | bytes accessed | tf_op | source)
XLA Modules:
  0.0 123.5 jit_solution(164977978223005825)
XLA Ops:
  1.3 0.0 copy-start
  1.3 0.9 copy-done
  2.2 0.0 copy-start.1
  2.2 0.9 copy-done.1
  3.2 0.0 copy-start.2
  3.2 0.7 copy-done.2
  3.9 114.5 %muon.1 = (f32[128,512]{1,0:T(8,128)S(1)}, f32[128,512]{1,0:T(8,128)S(1)}, bf16[8,4,128,512]{3,2,1,0:T(8,128)(2,1)S(1)}, f32[1]{0:T(128)}) custom-call(bf16[8,4,128,512]{3,2,1,0:T(8,128)(2,1)} %bitcast.3, f32[128,512]{1,0:T(8,128)S(1)} %copy-done, f32[128,512]{1,0:T(8,128)S(1)} %copy-done.1, s32[1,2,64]{2,1,0:T(2,128)S(1)} %copy-done.2, s32[1]{0:T(128)S(6)} %copy.13.threshold), custom_call_target="tpu_custom_call" | custom-call | tf_op jit(solution)/shard_map/muon/pallas_call | solution.py:587
  118.4 0.7 copy.14
  119.1 0.7 copy.15
  119.8 2.0 %copy.16 = bf16[4096,512]{1,0:T(8,128)(2,1)} copy(bf16[4096,512]{1,0:T(8,128)(2,1)S(1)} %bitcast.2) | data formatting | bytes 8388608
Async XLA Ops:
  1.3 1.0 copy-start
  2.2 0.9 copy-start.1
  3.2 0.7 copy-start.2

commit v7 on v6

--- a/solution.py
+++ b/solution.py
@@ -113,6 +113,7 @@
     ml_x,
     ml_mid,
     ml_pair,
+    scale_out,
     ml_z,
     plane,
     s_local,
@@ -364,78 +365,6 @@
         )
     drain(sent[:])
     sent.extend([swap] + copies)
-    part = half_sum[piece_of(0, m16)]
-    for r in range(1, 16):
-        copies[r - 1].wait_recv()
-        part = part + group_in[r - 1]
-    mid[...] = part
-    row_in[z // 2] = part
-    copies = []
-    for k in range(1, 4):
-        copies.append(
-            send(mid, row_in.at[z // 2], s_g.at[15 + k], r_g.at[15 + k], at_z((z + 2 * k) % NZ))
-        )
-    for copy in copies:
-        copy.wait_recv()
-    sent.extend(copies)
-    here = piece_of(core, m16)
-    full[here] = (row_in[0] + row_in[1]) + (row_in[2] + row_in[3])
-    copies = []
-    for r in range(1, 16):
-        copies.append(
-            send(
-                full.at[here], full.at[here], s_g.at[18 + r], r_g.at[18 + r], at_group((m16 + r) % 16)
-            )
-        )
-    swaps = [send(full.at[here], full.at[here], s_g.at[34], r_g.at[34], partner)]
-    for r in range(1, 16):
-        copies[r - 1].wait_recv()
-        there = piece_of(core, (m16 + 16 - r) % 16)
-        swaps.append(send(full.at[there], full.at[there], s_g.at[34 + r], r_g.at[34 + r], partner))
-    for copy in swaps:
-        copy.wait_recv()
-    sent.extend(copies)
-    sent.extend(swaps)
-
-    rows = lax.broadcasted_iota(jnp.int32, (BLOCK, BLOCK), 0)
-    cols = lax.broadcasted_iota(jnp.int32, (BLOCK, BLOCK), 1)
-    diagonal = jnp.zeros((BLOCK, BLOCK), jnp.float32)
-    for low, (i, j) in enumerate(PAIRS):
-        if i == j:
-            block = full[low * BLOCK : (low + 1) * BLOCK]
-            diagonal = diagonal + jnp.where(rows == cols, block, 0.0)
-    square_total = jnp.sum(jnp.sum(diagonal, axis=0, keepdims=True), axis=1, keepdims=True)
-    inverse = 1.0 / (jnp.sqrt(square_total) + epsilon)
-    blend_rms[0] = jnp.sqrt(square_total * (1.0 / (F * R)))[0, 0]
-    for low, (i, j) in enumerate(PAIRS):
-        block = full[low * BLOCK : (low + 1) * BLOCK] * inverse * inverse
-        gram[i * BLOCK : (i + 1) * BLOCK, j * BLOCK : (j + 1) * BLOCK] = block
-        if i != j:
-            gram[j * BLOCK : (j + 1) * BLOCK, i * BLOCK : (i + 1) * BLOCK] = block.T
-    ortho[...] = ortho[...] * inverse
-
-    def step(count, k, carry):
-        now = halves(gram[...], count)
-        square = mirrored(now[:2], now[:2])
-        row_ids = lax.broadcasted_iota(jnp.int32, (R, R), 0)
-        col_ids = lax.broadcasted_iota(jnp.int32, (R, R), 1)
-        factor = halves(
-            jnp.where(row_ids == col_ids, coef_one, 0.0) + coef_two * gram[...] + coef_three * square,
-            count,
-        )
-        ortho[...] = split_product(halves(ortho[...], 2), factor[:2])
-        once = halves(mirrored(now, factor), count)
-        gram[...] = mirrored(once, factor)
-        return carry
-
-    lax.fori_loop(0, FINE, functools.partial(step, 3), 0)
-    lax.fori_loop(FINE, ITERS - 1, functools.partial(step, 2), 0)
-    now = halves(gram[...], 2)
-    first = ortho[...]
-    second = split_product(halves(first, 2), now)
-    third = split_product(halves(second, 2), now)
-    last = coef_one * first + coef_two * second + coef_three * third
-
     for copy in ml_sends:
         copy.wait_recv()
     peaks = ml_pair[...]
@@ -450,9 +379,82 @@
     limit = jnp.full((1, 1), threshold[0], jnp.int32).astype(jnp.float32)
     gamma = jnp.minimum(1.0, limit / peak.astype(jnp.float32))
     scale = jnp.where(jnp.full((1, 1), d % 2, jnp.int32) == 0, jnp.sqrt(gamma), 1.0)
+    scale_out[...] = jnp.broadcast_to(scale, (8, 128))
+    part = half_sum[piece_of(0, m16)]
+    for r in range(1, 16):
+        copies[r - 1].wait_recv()
+        part = part + group_in[r - 1]
+    mid[...] = part
+    row_in[z // 2] = part
+    copies = []
+    for k in range(1, 4):
+        copies.append(
+            send(mid, row_in.at[z // 2], s_g.at[15 + k], r_g.at[15 + k], at_z((z + 2 * k) % NZ))
+        )
+    for copy in copies:
+        copy.wait_recv()
+    sent.extend(copies)
+    here = piece_of(core, m16)
+    full[here] = (row_in[0] + row_in[1]) + (row_in[2] + row_in[3])
+    copies = []
+    for r in range(1, 16):
+        copies.append(
+            send(
+                full.at[here], full.at[here], s_g.at[18 + r], r_g.at[18 + r], at_group((m16 + r) % 16)
+            )
+        )
+    swaps = [send(full.at[here], full.at[here], s_g.at[34], r_g.at[34], partner)]
+    for r in range(1, 16):
+        copies[r - 1].wait_recv()
+        there = piece_of(core, (m16 + 16 - r) % 16)
+        swaps.append(send(full.at[there], full.at[there], s_g.at[34 + r], r_g.at[34 + r], partner))
+    for copy in swaps:
+        copy.wait_recv()
+    sent.extend(copies)
+    sent.extend(swaps)
+
+    rows = lax.broadcasted_iota(jnp.int32, (BLOCK, BLOCK), 0)
+    cols = lax.broadcasted_iota(jnp.int32, (BLOCK, BLOCK), 1)
+    diagonal = jnp.zeros((BLOCK, BLOCK), jnp.float32)
+    for low, (i, j) in enumerate(PAIRS):
+        if i == j:
+            block = full[low * BLOCK : (low + 1) * BLOCK]
+            diagonal = diagonal + jnp.where(rows == cols, block, 0.0)
+    square_total = jnp.sum(jnp.sum(diagonal, axis=0, keepdims=True), axis=1, keepdims=True)
+    inverse = 1.0 / (jnp.sqrt(square_total) + epsilon)
+    rms = jnp.sqrt(square_total * (1.0 / (F * R)))
+    for low, (i, j) in enumerate(PAIRS):
+        block = full[low * BLOCK : (low + 1) * BLOCK] * inverse * inverse
+        gram[i * BLOCK : (i + 1) * BLOCK, j * BLOCK : (j + 1) * BLOCK] = block
+        if i != j:
+            gram[j * BLOCK : (j + 1) * BLOCK, i * BLOCK : (i + 1) * BLOCK] = block.T
+    ortho[...] = ortho[...] * inverse
+
+    def step(count, k, carry):
+        now = halves(gram[...], count)
+        square = mirrored(now[:2], now[:2])
+        row_ids = lax.broadcasted_iota(jnp.int32, (R, R), 0)
+        col_ids = lax.broadcasted_iota(jnp.int32, (R, R), 1)
+        factor = halves(
+            jnp.where(row_ids == col_ids, coef_one, 0.0) + coef_two * gram[...] + coef_three * square,
+            count,
+        )
+        ortho[...] = split_product(halves(ortho[...], 2), factor[:2])
+        once = halves(mirrored(now, factor), count)
+        gram[...] = mirrored(once, factor)
+        return carry
+
+    lax.fori_loop(0, FINE, functools.partial(step, 3), 0)
+    lax.fori_loop(FINE, ITERS - 1, functools.partial(step, 2), 0)
+    now = halves(gram[...], 2)
+    first = ortho[...]
+    second = split_product(halves(first, 2), now)
+    third = split_product(halves(second, 2), now)
+    last = coef_one * first + coef_two * second + coef_three * third
+
     update = last * (0.2 * float(max(F, R)) ** 0.5)
     stepped = weight_in[...] * (1.0 - learn_rate * decay_rate) - learn_rate * update
-    master = stepped * scale
+    master = stepped * scale_out[0:1, 0:1]
     master_out[...] = master
     stores.append(pltpu.make_async_copy(master_out, new_master, s_local.at[6]))
     rounded[...] = master.astype(jnp.bfloat16)
@@ -525,6 +527,7 @@
     stores[1].start()
     stores[2].start()
     drain(sent[:])
+    blend_rms[0] = rms[0, 0]
     places = [z]
     for k in range(1, 4):
         places.extend([(z + NZ - k) % NZ, (z + k) % NZ])
@@ -624,6 +627,7 @@
             pltpu.VMEM((3, 8, 128), i32),
             pltpu.VMEM((8, 128), i32),
             pltpu.VMEM((8, 128), i32),
+            pltpu.VMEM((8, 128), f32),
             pltpu.VMEM((4, 8, 128), i32),
             pltpu.SemaphoreType.REGULAR,
             dma((8,)),

time: 124 us -> 123 us (level)
  no operation moved by 1% of the time
where the time goes in v7:
time: 123 us
  Pallas kernels  114 us (93%)
  local copies, waits for them, and re-layouts  5.99 us (5%)
  between operations  3.04 us (2%)
    pallas_call x1, Pallas kernels, local(): pl.pallas_call(kernel, out_shape=(jax.ShapeDtypeStruct((BLOCK, R), f32),...  114 us
    unnamed x9, local copies, waits for them, and re-layouts  5.99 us

profile of v7, /device:TPU:1, one launch (start us, length us, event | category | flops | bytes accessed | tf_op | source)
XLA Modules:
  0.0 122.8 jit_solution(16753155086969249291)
XLA Ops:
  1.3 0.0 copy-start
  1.3 0.9 copy-done
  2.2 0.0 copy-start.1
  2.2 0.9 copy-done.1
  3.2 0.0 copy-start.2
  3.2 0.7 copy-done.2
  3.9 113.8 %muon.1 = (f32[128,512]{1,0:T(8,128)S(1)}, f32[128,512]{1,0:T(8,128)S(1)}, bf16[8,4,128,512]{3,2,1,0:T(8,128)(2,1)S(1)}, f32[1]{0:T(128)}) custom-call(bf16[8,4,128,512]{3,2,1,0:T(8,128)(2,1)} %bitcast.3, f32[128,512]{1,0:T(8,128)S(1)} %copy-done, f32[128,512]{1,0:T(8,128)S(1)} %copy-done.1, s32[1,2,64]{2,1,0:T(2,128)S(1)} %copy-done.2, s32[1]{0:T(128)S(6)} %copy.13.threshold), custom_call_target="tpu_custom_call" | custom-call | tf_op jit(solution)/shard_map/muon/pallas_call | solution.py:590
  117.7 0.7 copy.14
  118.4 0.7 copy.15
  119.1 2.0 %copy.16 = bf16[4096,512]{1,0:T(8,128)(2,1)} copy(bf16[4096,512]{1,0:T(8,128)(2,1)S(1)} %bitcast.2) | data formatting | bytes 8388608
Async XLA Ops:
  1.3 1.0 copy-start
  2.2 0.9 copy-start.1
  3.2 0.7 copy-start.2
